TPU v7x, 512 devices: a whole 4x8x8 slice. The times are simulated.
512 devices in a mesh: cfg: 2 (over core), tower: 4 (over z_hi), seq: 64 (over z_lo, x, y).
Axes of the slice: x: 4, y: 8, z: 8 (z_hi: 4, z_lo: 2; z = z_hi * 2 + z_lo), core: 2. Of those that a mesh axis runs over, the one named last changes fastest.
Arguments:
- query_self: bfloat16 [2, 4096, 2048], P('cfg', ('tower', 'seq')), may hold values from -320 to 320
- query_cross: bfloat16 [2, 4096, 2048], P('cfg', ('tower', 'seq')), may hold values from -320 to 320
- key_vectors: bfloat16 [2, 4096, 2048], P('cfg', ('tower', 'seq')), may hold values from -13 to 13
- values: bfloat16 [2, 4096, 2048], P('cfg', ('tower', 'seq')), may hold values from -6 to 6
- positions: int32 [4096], P(('tower', 'seq')), may hold values from 0 to 155, as said below
- counts: int32 [256], replicated, may hold values from 8 to 16, as said below
- guidance: float32 [1], replicated, may hold values from 1.5 to 3.5
Outputs:
- guided: bfloat16 [4096, 2048], P(('tower', 'seq'), 'cfg')
Inputs may be any that keep to these rules, and one draw needn't show every extreme that they name: `positions`: integer times on one clock for video and audio tokens, never falling along the video tokens and along the audio tokens; the video tokens of one latent frame share a time. `counts`: valid tokens of each device; a device's slots beyond its count are padding.
All inputs are finite; a program needn't handle non-finite values.
Results may differ from a plain program's by a relative error of at most 0.029.
Values may be sent and summed in bfloat16 or wider, within the bound.
A program may use at most 64 MiB of HBM per device.

v0:
```python
import math

import jax
import jax.numpy as jnp
from jax import lax
from jax.sharding import PartitionSpec as P

HEADS = 16
DHEAD = 128


def rotate_heads(matrix, positions):
    token_count = matrix.shape[0]
    half_dim = DHEAD // 2
    frequency = 10000.0 ** (-(jnp.arange(half_dim, dtype=jnp.float32) * 2.0 / DHEAD))
    angles = positions.astype(jnp.float32)[:, None] * frequency[None, :]
    cosine = jnp.cos(angles)[:, None, :]
    sine_part = jnp.sin(angles)[:, None, :]
    heads_f32 = matrix.astype(jnp.float32).reshape(token_count, HEADS, DHEAD)
    front_half = heads_f32[..., :half_dim]
    back_half = heads_f32[..., half_dim:]
    rotated = jnp.concatenate(
        [front_half * cosine - back_half * sine_part, back_half * cosine + front_half * sine_part],
        axis=-1,
    )
    return rotated.reshape(token_count, HEADS * DHEAD).astype(jnp.bfloat16)


def attend_blocks(queries, key_rows, value_rows, key_mask, key_block):
    query_count, per_dev, head_dim = queries.shape
    piece_count = key_rows.shape[0] // key_block
    key_pieces = key_rows.reshape(piece_count, key_block, per_dev, head_dim)
    value_pieces = value_rows.reshape(piece_count, key_block, per_dev, head_dim)
    mask_pieces = key_mask.reshape(piece_count, key_block)
    scale_factor = 1.0 / math.sqrt(head_dim)
    start_state = (
        jnp.full((per_dev, query_count), -1e30, jnp.float32),
        jnp.zeros((per_dev, query_count), jnp.float32),
        jnp.zeros((per_dev, query_count, head_dim), jnp.float32),
    )

    def advance(running, pieces):
        highest, weight_sum, weighted = running
        key_piece, value_piece, mask_piece = pieces
        scores = (
            jnp.einsum("qhd,khd->hqk", queries, key_piece, preferred_element_type=jnp.float32)
            * scale_factor
        )
        scores = jnp.where(mask_piece[None, None, :], scores, -1e30)
        new_high = jnp.maximum(highest, jnp.max(scores, axis=2))
        weights = jnp.where(mask_piece[None, None, :], jnp.exp(scores - new_high[:, :, None]), 0.0)
        factor = jnp.exp(highest - new_high)
        weight_sum = weight_sum * factor + jnp.sum(weights, axis=2)
        weighted = weighted * factor[:, :, None] + jnp.einsum(
            "hqk,khd->hqd",
            weights.astype(jnp.bfloat16),
            value_piece,
            preferred_element_type=jnp.float32,
        )
        return ((new_high, weight_sum, weighted), None)

    final_state, ignored = lax.scan(advance, start_state, (key_pieces, value_pieces, mask_pieces))
    return final_state


def per_device(query_self, query_cross, key_vectors, values, positions, counts, guidance):
    n_seq = lax.axis_size("seq")
    n_tower = lax.axis_size("tower")
    tokens_here = query_self.shape[1]
    feature_count = query_self.shape[2]
    per_dev = max(HEADS // n_seq, 1)
    query_blocks = max(n_seq // HEADS, 1)
    groups = HEADS // per_dev
    head_width = per_dev * DHEAD
    block_rows = tokens_here // query_blocks
    key_block = tokens_here * min(n_seq, 16)
    tower_at = lax.axis_index("tower")
    seq_at = lax.axis_index("seq")
    is_audio = tower_at == n_tower - 1
    rot_self = rotate_heads(query_self[0], positions)
    rot_cross = rotate_heads(query_cross[0], positions)
    rot_keys = rotate_heads(key_vectors[0], positions)
    value_rows = values[0]
    count_table = counts.reshape(n_tower, n_seq)
    slot_valid = jnp.arange(tokens_here, dtype=jnp.int32)[None, None, :] < count_table[:, :, None]
    key_valid = slot_valid.reshape(n_tower, n_seq * tokens_here)

    def spread_queries(matrix):
        parts = matrix.reshape(query_blocks, block_rows, groups, head_width).transpose(2, 0, 1, 3)
        return parts.reshape(n_seq, 1, block_rows, head_width)

    def spread_keys(matrix, towers_here):
        parts = matrix.reshape(towers_here, tokens_here, groups, head_width).transpose(2, 0, 1, 3)
        parts = jnp.broadcast_to(
            parts[:, None], (groups, query_blocks, towers_here, tokens_here, head_width)
        )
        return parts.reshape(n_seq, towers_here, tokens_here, head_width)

    key_source, value_source = (
        lax.all_gather(rot_keys, "tower", axis=0, tiled=True),
        lax.all_gather(value_rows, "tower", axis=0, tiled=True),
    )
    towers_here = n_tower
    arrived = (
        lax.all_to_all(spread_queries(rot_self), "seq", split_axis=0, concat_axis=2, tiled=True),
        lax.all_to_all(spread_queries(rot_cross), "seq", split_axis=0, concat_axis=2, tiled=True),
        lax.all_to_all(
            spread_keys(key_source, towers_here), "seq", split_axis=0, concat_axis=2, tiled=True
        ),
        lax.all_to_all(
            spread_keys(value_source, towers_here), "seq", split_axis=0, concat_axis=2, tiled=True
        ),
    )
    query_count = n_seq * block_rows
    key_count = n_seq * tokens_here
    head_self = arrived[0].reshape(query_count, per_dev, DHEAD)
    head_cross = arrived[1].reshape(query_count, per_dev, DHEAD)
    key_all = arrived[2].reshape(n_tower, key_count, per_dev, DHEAD)
    value_all = arrived[3].reshape(n_tower, key_count, per_dev, DHEAD)
    video_query = jnp.where(is_audio, head_cross, head_self)
    audio_query = jnp.where(is_audio, head_self, head_cross)
    video_count = (n_tower - 1) * key_count
    video_state = attend_blocks(
        video_query,
        key_all[: n_tower - 1].reshape(video_count, per_dev, DHEAD),
        value_all[: n_tower - 1].reshape(video_count, per_dev, DHEAD),
        key_valid[: n_tower - 1].reshape(video_count),
        key_block,
    )
    audio_state = attend_blocks(
        audio_query, key_all[n_tower - 1], value_all[n_tower - 1], key_valid[n_tower - 1], key_block
    )
    combined = (
        video_state[2] / video_state[1][:, :, None] + audio_state[2] / audio_state[1][:, :, None]
    )
    block_heads = (
        combined.transpose(1, 0, 2).reshape(n_seq, block_rows, head_width).astype(jnp.bfloat16)
    )
    returned = lax.all_to_all(block_heads, "seq", split_axis=0, concat_axis=0, tiled=True)
    token_major = (
        returned.reshape(groups, query_blocks, block_rows, head_width)
        .transpose(1, 2, 0, 3)
        .reshape(tokens_here, feature_count)
    )
    own_count = count_table[tower_at, seq_at]
    own_valid = jnp.arange(tokens_here, dtype=jnp.int32) < own_count
    block_rows_kept = jnp.where(own_valid[:, None], token_major, jnp.zeros_like(token_major))
    block_f32 = block_rows_kept.astype(jnp.float32)
    scale_rows = lax.rsqrt(jnp.mean(block_f32 * block_f32, axis=1, keepdims=True) + 1e-06)
    normed = (block_f32 * scale_rows).astype(jnp.bfloat16)
    paired = lax.all_to_all(normed[None], "cfg", split_axis=2, concat_axis=0, tiled=True)
    conditional = paired[0].astype(jnp.float32)
    unconditional = paired[1].astype(jnp.float32)
    return (unconditional + guidance[0] * (conditional - unconditional)).astype(jnp.bfloat16)


def solution(mesh):
    return jax.shard_map(
        per_device,
        mesh=mesh,
        in_specs=(
            P("cfg", ("tower", "seq"), None),
            P("cfg", ("tower", "seq"), None),
            P("cfg", ("tower", "seq"), None),
            P("cfg", ("tower", "seq"), None),
            P(("tower", "seq")),
            P(),
            P(),
        ),
        out_specs=P(("tower", "seq"), "cfg"),
        check_vma=False,
    )
```

profile of v0, /device:TPU:1, one launch (start us, length us, event | category | flops | bytes accessed | tf_op | source)
XLA Modules:
  0.0 181.6 jit_solution(16503542522304736761)
XLA Ops:
  0.0 0.6 copy-done.6
  0.7 0.8 convert_bitcast_fusion
  1.6 0.8 copy-done.1
  2.4 0.8 copy-done.2
  3.7 0.6 copy.43
  4.3 12.9 %all-to-all-start.1 = ((bf16[64,1,4,128]{3,2,1,0:T(4,128)(2,1)}), bf16[64,1,4,128]{3,2,1,0:T(4,128)(2,1)S(1)}, u32[]{:S(2)}, u32[]{:S(2)}) async-start(bf16[64,1,4,128]{3,2,1,0:T(4,128)(2,1)} %bitcast.9), calls=%async_computation.1 | async-start | bytes 131072 | tf_op jit(solution)/shard_map/all_to_all | solution.py:106
  17.4 0.6 copy.44
  18.2 17.1 %all-gather = bf16[1,64,2048]{2,1,0:T(8,128)(2,1)S(1)} all-gather(bf16[1,16,2048]{2,1,0:T(8,128)(2,1)S(1)} %copy-done.3), channel_id=2, replica_groups=mesh['cfg'=2,'tower'=4,'seq'=64] {'tower'}, dimensions={1}, use_global_device_ids=true | all-gather | bytes 327680 | tf_op jit(solution)/shard_map/all_gather | solution.py:101
  35.4 10.8 %all-to-all-start.2 = ((bf16[64,1,4,128]{3,2,1,0:T(4,128)(2,1)}), bf16[64,1,4,128]{3,2,1,0:T(4,128)(2,1)S(1)}, u32[]{:S(2)}, u32[]{:S(2)}) async-start(bf16[64,1,4,128]{3,2,1,0:T(4,128)(2,1)} %bitcast.12), calls=%async_computation.2 | async-start | bytes 131072 | tf_op jit(solution)/shard_map/all_to_all | solution.py:105
  46.3 9.4 %all-to-all-done.2 = bf16[64,1,4,128]{3,2,1,0:T(4,128)(2,1)S(1)} async-done(((bf16[64,1,4,128]{3,2,1,0:T(4,128)(2,1)}), bf16[64,1,4,128]{3,2,1,0:T(4,128)(2,1)S(1)}, u32[]{:S(2)}, u32[]{:S(2)}) %all-to-all-start.2) | async-done | bytes 65568 | tf_op jit(solution)/shard_map/all_to_all | solution.py:105
  55.7 1.2 broadcast_in_dim.95
  56.9 4.7 %all-to-all-start.3 = ((bf16[64,4,16,128]{3,2,1,0:T(8,128)(2,1)}), bf16[64,4,16,128]{3,2,1,0:T(8,128)(2,1)S(1)}, u32[]{:S(2)}, u32[]{:S(2)}) async-start(bf16[64,4,16,128]{3,2,1,0:T(8,128)(2,1)} %bitcast.15), calls=%async_computation.3 | async-start | bytes 2097152 | tf_op jit(solution)/shard_map/all_to_all | solution.py:110
  61.6 14.2 %all_gather.6 = bf16[64,2048]{1,0:T(8,128)(2,1)S(1)} all-gather(bf16[16,2048]{1,0:T(8,128)(2,1)S(1)} %bitcast.188), channel_id=1, replica_groups=mesh['cfg'=2,'tower'=4,'seq'=64] {'tower'}, dimensions={0}, use_global_device_ids=true | all-gather | bytes 327680 | tf_op jit(solution)/shard_map/all_gather | solution.py:100
  76.0 9.9 %all-to-all-done.3 = bf16[64,4,16,128]{3,2,1,0:T(8,128)(2,1)S(1)} async-done(((bf16[64,4,16,128]{3,2,1,0:T(8,128)(2,1)}), bf16[64,4,16,128]{3,2,1,0:T(8,128)(2,1)S(1)}, u32[]{:S(2)}, u32[]{:S(2)}) %all-to-all-start.3) | async-done | bytes 1048608 | tf_op jit(solution)/shard_map/all_to_all | solution.py:110
  85.9 1.2 broadcast_in_dim.94
  87.1 6.6 %all-to-all-start = ((bf16[64,4,16,128]{3,2,1,0:T(8,128)(2,1)}), bf16[64,4,16,128]{3,2,1,0:T(8,128)(2,1)S(1)}, u32[]{:S(2)}, u32[]{:S(2)}) async-start(bf16[64,4,16,128]{3,2,1,0:T(8,128)(2,1)} %bitcast.2), calls=%async_computation | async-start | bytes 2097152 | tf_op jit(solution)/shard_map/all_to_all | solution.py:107
  93.8 0.7 copy-done.5
  94.7 0.6 copy-done
  95.3 0.7 reshape_reshape.9
  96.0 0.7 reshape_squeeze.9
  96.6 0.6 dynamic_slice.25
  97.7 19.8 %all-to-all-done = bf16[64,4,16,128]{3,2,1,0:T(8,128)(2,1)S(1)} async-done(((bf16[64,4,16,128]{3,2,1,0:T(8,128)(2,1)}), bf16[64,4,16,128]{3,2,1,0:T(8,128)(2,1)S(1)}, u32[]{:S(2)}, u32[]{:S(2)}) %all-to-all-start) | async-done | bytes 1048608 | tf_op jit(solution)/shard_map/all_to_all | solution.py:107
  117.9 0.7 copy-done.4
  118.5 3.0 %while.31 = (s32[]{:T(128)}, f32[1,256]{1,0:T(1,128)S(1)}, f32[1,256]{1,0:T(1,128)S(1)}, f32[1,256,128]{2,1,0:T(8,128)S(1)}, pred[4,256]{1,0:T(4,128)(4,1)S(1)},...) while((s32[]{:T(128)}, f32[1,256]{1,0:T(1,128)S(1)}, ...), condition=%wide.region_7.8_spmd.clone, body=%wide.region_4.7_spmd.clone.sunk | while | flops 34243840 | bytes 1263493 | solution.py:62
  118.9 0.3 fusion.70
  119.7 0.3 fusion.70
  120.4 0.3 fusion.70
  121.2 0.3 fusion.70
  121.5 17.1 %while.30 = (s32[]{:T(128)}, f32[1,256]{1,0:T(1,128)S(1)}, f32[1,256]{1,0:T(1,128)S(1)}, f32[1,256,128]{2,1,0:T(8,128)S(1)}, pred[12,256]{1,0:T(8,128)(4,1)}, /*...) while((s32[]{:T(128)}, f32[1,256]{1,0:T(1,128)S(1)}, ...), condition=%wide.region_3.4_spmd.clone, body=%wide.region_0.3_spmd.clone.sunk | while | flops 34243840 | bytes 1263493 | solution.py:62
  121.6 0.7 dynamic-slice_reduce_fusion.4
  122.6 0.3 fusion.63
  123.0 0.7 dynamic-slice_reduce_fusion.4
  124.0 0.3 fusion.63
  124.4 0.7 dynamic-slice_reduce_fusion.4
  125.8 0.7 dynamic-slice_reduce_fusion.4
  126.9 0.3 fusion.63
  127.2 0.7 dynamic-slice_reduce_fusion.4
  128.6 0.7 dynamic-slice_reduce_fusion.4
  129.7 0.3 fusion.63
  130.1 0.7 dynamic-slice_reduce_fusion.4
  131.1 0.3 fusion.63
  131.5 0.7 dynamic-slice_reduce_fusion.4
  132.6 0.3 fusion.63
  132.9 0.7 dynamic-slice_reduce_fusion.4
  134.0 0.3 fusion.63
  134.3 0.7 dynamic-slice_reduce_fusion.4
  135.4 0.3 fusion.63
  135.8 0.7 dynamic-slice_reduce_fusion.4
  136.8 0.3 fusion.63
  137.2 0.7 dynamic-slice_reduce_fusion.4
  138.3 0.3 fusion.63
  138.6 0.8 add_convert_fusion
  139.4 6.6 %all-to-all-start.4 = ((bf16[64,4,128]{2,1,0:T(4,128)(2,1)}), bf16[64,4,128]{2,1,0:T(4,128)(2,1)S(1)}, u32[]{:S(2)}, u32[]{:S(2)}) async-start(bf16[64,4,128]{2,1,0:T(4,128)(2,1)} %bitcast.29), calls=%async_computation.4 | async-start | bytes 131072 | tf_op jit(solution)/shard_map/all_to_all | solution.py:139
  146.0 0.6 add_compare_fusion
  147.3 0.6 iota_compare_fusion.1
  147.9 7.4 %all-to-all-done.4 = bf16[64,4,128]{2,1,0:T(4,128)(2,1)S(1)} async-done(((bf16[64,4,128]{2,1,0:T(4,128)(2,1)}), bf16[64,4,128]{2,1,0:T(4,128)(2,1)S(1)}, u32[]{:S(2)}, u32[]{:S(2)}) %all-to-all-start.4) | async-done | bytes 65568 | tf_op jit(solution)/shard_map/all_to_all | solution.py:139
  155.9 0.7 copy.54
  156.7 0.5 broadcast.279
  157.2 11.5 %reduce.17 = bf16[2048,16]{1,0:T(8,128)(2,1)S(1)} reduce(bf16[2048,1,16]{2,1,0:T(2,128)(2,1)S(1)} %bitcast.162, bf16[]{:T(256)} %broadcast.279), dimensions={1}, to_apply=%bitcast.114.reduce_sub_computation | reduce | bytes 131074
  168.7 0.5 reshape.363
  169.3 10.3 %all_to_all.68 = bf16[2,2,8192]{2,1,0:T(2,128)(2,1)S(1)} all-to-all(bf16[2,2,8192]{2,1,0:T(2,128)(2,1)S(1)} %reshape.363), channel_id=1, replica_groups=mesh['cfg'=2,'tower'=4,'seq'=64] {'cfg'}, dimensions={0} | all-to-all | bytes 131072 | tf_op jit(solution)/shard_map/all_to_all | solution.py:151
  179.6 0.8 reshape.364
  180.3 0.5 copy.55
  181.0 0.6 fusion.39
  (141 shorter events, 9.3 us)
Async XLA Ops:
  0.0 0.7 copy-start.6
  1.5 0.8 copy-start.1
  2.4 0.8 copy-start.2
  4.3 31.0 %all-to-all-start.1 = ((bf16[64,1,4,128]{3,2,1,0:T(4,128)(2,1)}), bf16[64,1,4,128]{3,2,1,0:T(4,128)(2,1)S(1)}, u32[]{:S(2)}, u32[]{:S(2)}) async-start(bf16[64,1,4,128]{3,2,1,0:T(4,128)(2,1)} %bitcast.9), calls=%async_computation.1 | async-start | bytes 131072 | tf_op jit(solution)/shard_map/all_to_all | solution.py:106
  17.4 0.8 copy-start.3
  35.4 20.3 %all-to-all-start.2 = ((bf16[64,1,4,128]{3,2,1,0:T(4,128)(2,1)}), bf16[64,1,4,128]{3,2,1,0:T(4,128)(2,1)S(1)}, u32[]{:S(2)}, u32[]{:S(2)}) async-start(bf16[64,1,4,128]{3,2,1,0:T(4,128)(2,1)} %bitcast.12), calls=%async_computation.2 | async-start | bytes 131072 | tf_op jit(solution)/shard_map/all_to_all | solution.py:105
  56.9 29.0 %all-to-all-start.3 = ((bf16[64,4,16,128]{3,2,1,0:T(8,128)(2,1)}), bf16[64,4,16,128]{3,2,1,0:T(8,128)(2,1)S(1)}, u32[]{:S(2)}, u32[]{:S(2)}) async-start(bf16[64,4,16,128]{3,2,1,0:T(8,128)(2,1)} %bitcast.15), calls=%async_computation.3 | async-start | bytes 2097152 | tf_op jit(solution)/shard_map/all_to_all | solution.py:110
  87.1 30.4 %all-to-all-start = ((bf16[64,4,16,128]{3,2,1,0:T(8,128)(2,1)}), bf16[64,4,16,128]{3,2,1,0:T(8,128)(2,1)S(1)}, u32[]{:S(2)}, u32[]{:S(2)}) async-start(bf16[64,4,16,128]{3,2,1,0:T(8,128)(2,1)} %bitcast.2), calls=%async_computation | async-start | bytes 2097152 | tf_op jit(solution)/shard_map/all_to_all | solution.py:107
  93.8 0.7 copy-start.5
  94.6 0.6 copy-start
  95.3 0.7 slice-start
  117.9 0.7 copy-start.4
  139.4 16.0 %all-to-all-start.4 = ((bf16[64,4,128]{2,1,0:T(4,128)(2,1)}), bf16[64,4,128]{2,1,0:T(4,128)(2,1)S(1)}, u32[]{:S(2)}, u32[]{:S(2)}) async-start(bf16[64,4,128]{2,1,0:T(4,128)(2,1)} %bitcast.29), calls=%async_computation.4 | async-start | bytes 131072 | tf_op jit(solution)/shard_map/all_to_all | solution.py:139
where the time goes:
time: 183 us; the launch traced here: 182 us
  waiting for transfers between devices  46.6 us (25%)
  starting transfers between devices  41.6 us (23%)
  blocking collectives  41.6 us (23%)
  local copies, waits for them, and re-layouts  23.1 us (13%)
  other arithmetic  18.5 us (10%)
  matrix products  8.61 us (5%)
    all_to_all x1, waiting for transfers between devices, per_device(): lax.all_to_all(spread_keys(key_source, towers_here), 'seq', split_axis=0,...  19.8 us
    all_gather x1, blocking collectives, per_device(): lax.all_gather(value_rows, 'tower', axis=0, tiled=True)  17.1 us
    all_gather x1, blocking collectives, per_device(): lax.all_gather(rot_keys, 'tower', axis=0, tiled=True)  14.2 us
    all_to_all x1, starting transfers between devices, per_device(): lax.all_to_all(spread_queries(rot_cross), 'seq', split_axis=0, concat_axi...  12.9 us
    unnamed x10, other arithmetic  12.4 us
    all_to_all x1, starting transfers between devices, per_device(): lax.all_to_all(spread_queries(rot_self), 'seq', split_axis=0, concat_axis...  10.8 us
    all_to_all x1, blocking collectives, per_device(): lax.all_to_all(normed[None], 'cfg', split_axis=2, concat_axis=0, tiled=True)  10.3 us
    all_to_all x1, waiting for transfers between devices, per_device(): lax.all_to_all(spread_keys(value_source, towers_here), 'seq', split_axis=...  9.93 us
  transfers between devices with their start and end apart: 5, of which 4 were waited for; matrix products, arithmetic and copies ran while one was open for 3% of the time, Pallas kernels for 0%

commit v1 on v0

v1 whole, which is shorter than its diff:
```python
import math

import jax
import jax.numpy as jnp
from jax import lax
from jax.experimental import pallas as pl
from jax.experimental.pallas import tpu as pltpu
from jax.sharding import PartitionSpec as P

HEADS = 16
D = 128
TOK = 16
SCALE = 1.0 / math.sqrt(D)
MESH = pl.DeviceIdType.MESH


def loop(lo, hi, fn):
    def body(k, carry):
        fn(k)
        return carry

    lax.fori_loop(lo, hi, body, 0)


def device(x, y, z):
    return {"tower": z // 2, "seq": (z % 2) * 32 + x * 8 + y}


def kernel(
    qs_hbm, qc_hbm, k_hbm, v_hbm, pos_hbm, counts_hbm, guide_hbm,
    out_ref,
    raw, pos, counts, guide, ones,
    kv_send, kv_all, q_rot, q_z, q_all, o_send, o_recv, l_send, l_recv, normed, paired,
    load_sem, send_sem, recv_sem,
):
    cfg = lax.axis_index("cfg")
    tower = lax.axis_index("tower")
    seq = lax.axis_index("seq")
    zl, x, y = seq // 32, (seq // 8) % 4, seq % 8
    z = tower * 2 + zl

    def lo_peer(k):
        return (y + k // 2) % 8, (zl + k % 2) % 2

    def signal(target):
        pl.semaphore_signal(barrier, inc=1, device_id=target, device_id_type=MESH)

    def remote(src, dst, target, stage):
        pltpu.make_async_remote_copy(
            src_ref=src, dst_ref=dst,
            send_sem=send_sem.at[stage], recv_sem=recv_sem.at[stage],
            device_id=target, device_id_type=MESH,
        ).start()

    def local(src, dst, stage):
        pltpu.make_async_copy(src, dst, recv_sem.at[stage]).start()

    def arrived(like, stage):
        pltpu.make_async_copy(like, like, recv_sem.at[stage]).wait()

    def sent(like, stage):
        pltpu.make_async_copy(like, like, send_sem.at[stage]).wait()

    barrier = pltpu.get_barrier_semaphore()

    def greet_lo(k):
        y2, zl2 = lo_peer(k)
        signal(device(x, y2, tower * 2 + zl2))

    loop(1, 16, greet_lo)
    loop(1, 8, lambda k: signal(device(x, y, (z + k) % 8)))
    loop(1, 4, lambda k: signal(device((x + k) % 4, y, z)))
    signal({"cfg": 1 - cfg})

    loads = [
        pltpu.make_async_copy(pos_hbm, pos, load_sem.at[4]),
        pltpu.make_async_copy(counts_hbm, counts, load_sem.at[5]),
        pltpu.make_async_copy(k_hbm, raw.at[2], load_sem.at[2]),
        pltpu.make_async_copy(v_hbm, raw.at[3], load_sem.at[3]),
        pltpu.make_async_copy(qs_hbm, raw.at[0], load_sem.at[0]),
        pltpu.make_async_copy(qc_hbm, raw.at[1], load_sem.at[1]),
        pltpu.make_async_copy(guide_hbm, guide, load_sem.at[6]),
    ]
    for copy in loads:
        copy.start()
    for copy in loads:
        copy.wait()

    row = lax.broadcasted_iota(jnp.int32, (TOK, D), 0)
    lane = lax.broadcasted_iota(jnp.int32, (TOK, D), 1)
    time = jnp.zeros((TOK, D), jnp.int32)
    for i in range(TOK):
        time = jnp.where(row == i, pos[i], time)
    half = (lane % 64).astype(jnp.float32)
    frequency = jnp.exp(half * (-2.0 / D * math.log(10000.0)))
    angle = time.astype(jnp.float32) * frequency
    cosine = jnp.cos(angle)
    sine = jnp.where(lane < 64, -jnp.sin(angle), jnp.sin(angle))

    def rope(which, h):
        block = raw[which, :, h * D:(h + 1) * D].astype(jnp.float32)
        return block * cosine + pltpu.roll(block, 64, axis=1) * sine

    own_valid = row < counts[tower * 64 + seq]
    for h in range(HEADS):
        keys = rope(2, h)
        kv_send[h, 0] = jnp.where(own_valid, keys, keys[0:1, :]).astype(jnp.bfloat16)
        vals = raw[3, :, h * D:(h + 1) * D]
        kv_send[h, 1] = jnp.where(own_valid, vals.astype(jnp.float32), 0.0).astype(jnp.bfloat16)
    for h in range(HEADS):
        q_rot[0, h % 2, h // 2] = rope(0, h).astype(jnp.bfloat16)
        q_rot[1, h % 2, h // 2] = rope(1, h).astype(jnp.bfloat16)

    pl.semaphore_wait(barrier, 15 + 7 + 3 + 1)

    own_slot = y * 2 + zl

    def send_kv(k):
        y2, zl2 = lo_peer(k)
        remote(kv_send.at[y2 * 2 + zl2], kv_all.at[x, own_slot], device(x, y2, tower * 2 + zl2), 0)

    def q_for(z2):
        return q_rot.at[(z // 6 + z2 // 6) % 2, z2 % 2]

    def send_q(k):
        z2 = (z + k) % 8
        remote(q_for(z2), q_z.at[z], device(x, y, z2), 1)

    local(kv_send.at[own_slot], kv_all.at[x, own_slot], 0)
    local(q_for(z), q_z.at[z], 1)
    loop(1, 16, send_kv)
    loop(1, 8, send_q)

    def flags(i):
        count = counts[tower * 64 + (i % 2) * 32 + (i // 16) * 8 + (i // 2) % 8]
        ones[i] = jnp.where(row < count, 1.0, 0.0).astype(jnp.bfloat16)

    loop(0, 64, flags)

    arrived(kv_all.at[x], 0)
    for k in (2, 1, 3):
        remote(kv_all.at[x], kv_all.at[x], device((x + k) % 4, y, z), 2)
    arrived(q_z, 1)

    def pass_q(k):
        y2 = (y + k) % 8
        remote(q_z.at[:, y2], q_all.at[y], device(x, y2, z), 3)

    local(q_z.at[:, y], q_all.at[y], 3)
    loop(1, 8, pass_q)
    arrived(kv_all.at[pl.ds(0, 3)], 2)
    arrived(q_all, 3)

    slot = tower * HEADS + own_slot

    def attend(step):
        y2 = (y + 4 + ((step + 1) // 2) * (2 * (step % 2) - 1)) % 8
        queries = q_all[y2].reshape(8 * TOK, D)
        keys = kv_all[:, :, 0].reshape(64 * TOK, D)
        values = jnp.concatenate(
            [kv_all[:, :, 1].reshape(64 * TOK, D), ones[...].reshape(64 * TOK, D)], axis=1
        )
        scores = lax.dot_general(
            queries, keys, (((1,), (1,)), ((), ())), preferred_element_type=jnp.float32
        )
        highest = jnp.max(scores, axis=1, keepdims=True)
        weights = jnp.exp2((scores - highest) * (SCALE / math.log(2.0))).astype(jnp.bfloat16)
        total = jnp.dot(weights, values, preferred_element_type=jnp.float32)
        weight_sum = total[:, D:]
        o_send[y2] = (total[:, :D] / weight_sum).astype(jnp.bfloat16).reshape(8, TOK, D)
        level = highest * SCALE + jnp.log(weight_sum)
        l_send[y2] = jnp.transpose(level)[0:1, :]

        def send_out(k):
            z2 = (z + 4 + k) % 8
            remote(l_send.at[y2], l_recv.at[slot], device(x, y2, z2), 5)
            remote(o_send.at[y2, z2], o_recv.at[slot], device(x, y2, z2), 4)

        loop(0, 4, send_out)
        loop(5, 8, send_out)
        return y2

    def attend_other(step):
        y2 = attend(step)
        remote(l_send.at[y2], l_recv.at[slot], device(x, y2, z), 5)
        remote(o_send.at[y2, z], o_recv.at[slot], device(x, y2, z), 4)

    loop(0, 7, attend_other)
    attend(7)
    local(l_send.at[y], l_recv.at[slot], 5)
    local(o_send.at[y, z], o_recv.at[slot], 4)

    arrived(l_recv, 5)
    levels = l_recv[...].reshape(64, D)
    levels = jnp.transpose(jnp.concatenate([levels, levels], axis=0))
    mine = jnp.zeros((TOK, D), jnp.float32)
    for z2 in range(8):
        mine = jnp.where(z == z2, levels[z2 * TOK:(z2 + 1) * TOK], mine)
    per_tower = [mine[:, t * HEADS:(t + 1) * HEADS] for t in range(3)]
    top = jnp.maximum(jnp.maximum(per_tower[0], per_tower[1]), per_tower[2])
    shares = [jnp.exp(level - top) for level in per_tower]
    share_sum = shares[0] + shares[1] + shares[2]
    shares = [share / share_sum for share in shares]
    arrived(o_recv, 4)
    blocks = []
    squares = jnp.zeros((TOK, D), jnp.float32)
    for h in range(HEADS):
        block = o_recv[3 * HEADS + h].astype(jnp.float32)
        for t in range(3):
            block += shares[t][:, h:h + 1] * o_recv[t * HEADS + h].astype(jnp.float32)
        block = jnp.where(own_valid, block, 0.0).astype(jnp.bfloat16).astype(jnp.float32)
        blocks.append(block)
        squares += block * block
    mean = jnp.sum(squares, axis=1, keepdims=True) * (1.0 / (HEADS * D))
    norm = lax.rsqrt(mean + 1e-06)
    for h in range(HEADS):
        normed[h] = (blocks[h] * norm).astype(jnp.bfloat16)

    half_heads = HEADS // 2
    remote(normed.at[pl.ds((1 - cfg) * half_heads, half_heads)], paired, {"cfg": 1 - cfg}, 6)
    arrived(paired, 6)
    for h in range(half_heads):
        here = normed[cfg * half_heads + h].astype(jnp.float32)
        there = paired[h].astype(jnp.float32)
        conditional = jnp.where(cfg == 0, here, there)
        unconditional = jnp.where(cfg == 0, there, here)
        guided = unconditional + guide[0] * (conditional - unconditional)
        out_ref[:, h * D:(h + 1) * D] = guided.astype(jnp.bfloat16)

    sent(kv_send.at[pl.ds(0, 15)], 0)
    sent(q_z.at[pl.ds(0, 7)], 1)
    sent(kv_all.at[pl.ds(0, 3)], 2)
    sent(q_all.at[pl.ds(0, 7)], 3)
    sent(o_recv.at[pl.ds(0, 63)], 4)
    sent(l_recv.at[pl.ds(0, 63)], 5)
    sent(paired, 6)


def per_device(query_self, query_cross, key_vectors, values, positions, counts, guidance):
    anywhere = pl.BlockSpec(memory_space=pl.ANY)
    bf16 = jnp.bfloat16
    return pl.pallas_call(
        kernel,
        out_shape=jax.ShapeDtypeStruct((TOK, HEADS * D // 2), bf16),
        in_specs=[anywhere] * 7,
        out_specs=pl.BlockSpec(memory_space=pltpu.VMEM),
        scratch_shapes=[
            pltpu.VMEM((4, TOK, HEADS * D), bf16),
            pltpu.SMEM((TOK,), jnp.int32),
            pltpu.SMEM((256,), jnp.int32),
            pltpu.SMEM((1,), jnp.float32),
            pltpu.VMEM((64, TOK, D), bf16),
            pltpu.VMEM((HEADS, 2, TOK, D), bf16),
            pltpu.VMEM((4, HEADS, 2, TOK, D), bf16),
            pltpu.VMEM((2, 2, 8, TOK, D), bf16),
            pltpu.VMEM((8, 8, TOK, D), bf16),
            pltpu.VMEM((8, 8, TOK, D), bf16),
            pltpu.VMEM((8, 8, TOK, D), bf16),
            pltpu.VMEM((64, TOK, D), bf16),
            pltpu.VMEM((8, 1, D), jnp.float32),
            pltpu.VMEM((64, 1, D), jnp.float32),
            pltpu.VMEM((HEADS, TOK, D), bf16),
            pltpu.VMEM((HEADS // 2, TOK, D), bf16),
            pltpu.SemaphoreType.DMA((7,)),
            pltpu.SemaphoreType.DMA((7,)),
            pltpu.SemaphoreType.DMA((7,)),
        ],
        compiler_params=pltpu.CompilerParams(
            collective_id=0, has_side_effects=True, vmem_limit_bytes=32 * 1024 * 1024
        ),
        name="twin_attention",
    )(query_self[0], query_cross[0], key_vectors[0], values[0], positions, counts, guidance)


def solution(mesh):
    return jax.shard_map(
        per_device,
        mesh=mesh,
        in_specs=(
            P("cfg", ("tower", "seq"), None),
            P("cfg", ("tower", "seq"), None),
            P("cfg", ("tower", "seq"), None),
            P("cfg", ("tower", "seq"), None),
            P(("tower", "seq")),
            P(),
            P(),
        ),
        out_specs=P(("tower", "seq"), "cfg"),
        check_vma=False,
    )
```

time: 183 us -> 53 us (0.29)
  Pallas kernels: 0 us -> 47.3 us
  waiting for transfers between devices: 46.6 us -> 0 us
  blocking collectives: 41.6 us -> 0 us
  starting transfers between devices: 41.6 us -> 0 us
  other arithmetic: 18.5 us -> 0 us
  local copies, waits for them, and re-layouts: 23.1 us -> 4.64 us
  matrix products: 8.61 us -> 0 us
    pallas_call x0 -> x1, Pallas kernels: none -> 47.3 us  [per_device(): pl.pallas_call(kernel, out_shape=jax.ShapeDtypeStruct((TOK, HEADS * D //...]
    all_to_all x5 -> x0, waiting for transfers between devices: 46.6 us -> none  [the longest x1 19.8 us: per_device(): lax.all_to_all(spread_keys(key_source, towers_here), 'seq', split_axis=0,...]
    all_to_all x5 -> x0, starting transfers between devices: 41.6 us -> none  [the longest x1 12.9 us: per_device(): lax.all_to_all(spread_queries(rot_cross), 'seq', split_axis=0, concat_axi...]
    all_gather x2 -> x0, blocking collectives: 31.3 us -> none  [the longest x1 17.1 us: per_device(): lax.all_gather(value_rows, 'tower', axis=0, tiled=True)]
    unnamed x10 -> x0, other arithmetic: 12.4 us -> none
    all_to_all x1 -> x0, blocking collectives: 10.3 us -> none  [per_device(): lax.all_to_all(normed[None], 'cfg', split_axis=2, concat_axis=0, tiled=True)]
    dynamic_slice x17 -> x0, local copies, waits for them, and re-layouts: 9.15 us -> none  [the longest x16 8.5 us: attend_blocks(): lax.scan(advance, start_state, (key_pieces, value_pieces, mask_pieces))]
    dot_general x32 -> x0, matrix products: 8.61 us -> none  [the longest x16 5.13 us: advance(): jnp.einsum('hqk,khd->hqd', weights.astype(jnp.bfloat16), value_piece, pre...]
  transfers between devices with their start and end apart: 5 -> 0, of which waited for: 4 -> 0; matrix products, arithmetic and copies ran while one was open for 3% -> 0% of each run, Pallas kernels for 0% -> 0%
where the time goes in v1:
time: 53 us; the launch traced here: 52.6 us
  Pallas kernels  47.3 us (89%)
  local copies, waits for them, and re-layouts  4.64 us (9%)
  between operations  0.68 us (1%)
    pallas_call x1, Pallas kernels, per_device(): pl.pallas_call(kernel, out_shape=jax.ShapeDtypeStruct((TOK, HEADS * D //...  47.3 us
    unnamed x13, local copies, waits for them, and re-layouts  4.64 us

profile of v1, /device:TPU:1, one launch (start us, length us, event | category | flops | bytes accessed | tf_op | source)
XLA Modules:
  0.0 52.6 jit_solution(9702260354289014630)
XLA Ops:
  0.7 0.0 copy-start.4
  0.7 0.0 copy-start.5
  0.7 0.7 %copy-done.4 = s32[256]{0:T(256)S(1)} copy-done((s32[256]{0:T(256)S(1)}, s32[256]{0:T(256)}, u32[]{:S(2)}) %copy-start.4) | copy-done | bytes 1048
  1.3 0.0 copy-done.5
  1.3 0.0 copy-start
  1.3 0.8 %copy-done = bf16[1,16,2048]{2,1,0:T(8,128)(2,1)S(1)} copy-done((bf16[1,16,2048]{2,1,0:T(8,128)(2,1)S(1)}, bf16[1,16,2048]{2,1,0:T(8,128)(2,1)}, u32[]{:S(2)}) %copy-start) | copy-done | bytes 65560
  2.2 0.0 copy-start.1
  2.2 0.8 %copy-done.1 = bf16[1,16,2048]{2,1,0:T(8,128)(2,1)S(1)} copy-done((bf16[1,16,2048]{2,1,0:T(8,128)(2,1)S(1)}, bf16[1,16,2048]{2,1,0:T(8,128)(2,1)}, u32[]{:S(2)}) %copy-start.1) | copy-done | bytes 65560
  3.0 0.0 copy-start.2
  3.0 0.8 %copy-done.2 = bf16[1,16,2048]{2,1,0:T(8,128)(2,1)S(1)} copy-done((bf16[1,16,2048]{2,1,0:T(8,128)(2,1)S(1)}, bf16[1,16,2048]{2,1,0:T(8,128)(2,1)}, u32[]{:S(2)}) %copy-start.2) | copy-done | bytes 65560
  3.9 0.0 copy-start.3
  3.9 0.8 %copy-done.3 = bf16[1,16,2048]{2,1,0:T(8,128)(2,1)S(1)} copy-done((bf16[1,16,2048]{2,1,0:T(8,128)(2,1)S(1)}, bf16[1,16,2048]{2,1,0:T(8,128)(2,1)}, u32[]{:S(2)}) %copy-start.3) | copy-done | bytes 65560
  4.7 47.3 %twin_attention.1 = bf16[16,1024]{1,0:T(8,128)(2,1)S(1)} custom-call(bf16[16,2048]{1,0:T(8,128)(2,1)S(1)} %bitcast.4, bf16[16,2048]{1,0:T(8,128)(2,1)S(1)} %bitcast.5, bf16[16,2048]{1,0:T(8,128)(2,1)S(1)} %bitcast.6, bf16[16,2048]{1,0:T(8,128)(2,1)S(1)} %bitcast.7, s32[16]{0:T(128)S(1)} %copy-done.5, s32[256]{0:T(256)S(1)} %copy-done.4, f32[1]{0:T(128)S(6)} %copy.9.guide_hbm), custom_call_target="tpu_custom_call" | custom-call | tf_op jit(solution)/shard_map/twin_attention/pallas_call | solution.py:242
  52.0 0.6 %copy.10 = bf16[16,1024]{1,0:T(8,128)(2,1)} copy(bf16[16,1024]{1,0:T(8,128)(2,1)S(1)} %twin_attention.1) | data formatting | bytes 65536
Async XLA Ops:
  0.7 0.7 %copy-start.4 = (s32[256]{0:T(256)S(1)}, s32[256]{0:T(256)}, u32[]{:S(2)}) copy-start(s32[256]{0:T(256)} %counts_hbm.1) | copy-start | bytes 3076
  0.7 0.7 %copy-start.5 = (s32[16]{0:T(128)S(1)}, s32[16]{0:T(128)}, u32[]{:S(2)}) copy-start(s32[16]{0:T(128)} %pos_hbm.1) | copy-start | bytes 196
  1.3 0.8 %copy-start = (bf16[1,16,2048]{2,1,0:T(8,128)(2,1)S(1)}, bf16[1,16,2048]{2,1,0:T(8,128)(2,1)}, u32[]{:S(2)}) copy-start(bf16[1,16,2048]{2,1,0:T(8,128)(2,1)} %param.7) | copy-start | bytes 196612
  2.2 0.8 %copy-start.1 = (bf16[1,16,2048]{2,1,0:T(8,128)(2,1)S(1)}, bf16[1,16,2048]{2,1,0:T(8,128)(2,1)}, u32[]{:S(2)}) copy-start(bf16[1,16,2048]{2,1,0:T(8,128)(2,1)} %param.8) | copy-start | bytes 196612
  3.0 0.8 %copy-start.2 = (bf16[1,16,2048]{2,1,0:T(8,128)(2,1)S(1)}, bf16[1,16,2048]{2,1,0:T(8,128)(2,1)}, u32[]{:S(2)}) copy-start(bf16[1,16,2048]{2,1,0:T(8,128)(2,1)} %param.9) | copy-start | bytes 196612
  3.9 0.8 %copy-start.3 = (bf16[1,16,2048]{2,1,0:T(8,128)(2,1)S(1)}, bf16[1,16,2048]{2,1,0:T(8,128)(2,1)}, u32[]{:S(2)}) copy-start(bf16[1,16,2048]{2,1,0:T(8,128)(2,1)} %param.10) | copy-start | bytes 196612

commit v2 on v1

--- a/solution.py
+++ b/solution.py
@@ -30,7 +30,7 @@
     qs_hbm, qc_hbm, k_hbm, v_hbm, pos_hbm, counts_hbm, guide_hbm,
     out_ref,
     raw, pos, counts, guide, ones,
-    kv_send, kv_all, q_rot, q_z, q_all, o_send, o_recv, l_send, l_recv, normed, paired,
+    kv_send, kv_all, q_rot, q_z, q_all, keys_t, o_send, o_recv, l_send, l_recv, normed, paired,
     load_sem, send_sem, recv_sem,
 ):
     cfg = lax.axis_index("cfg")
@@ -153,16 +153,14 @@
 
     slot = tower * HEADS + own_slot
 
-    def attend(step):
-        y2 = (y + 4 + ((step + 1) // 2) * (2 * (step % 2) - 1)) % 8
+    keys_t[...] = jnp.transpose(kv_all[:, :, 0].reshape(64 * TOK, D))
+
+    def attend(y2):
         queries = q_all[y2].reshape(8 * TOK, D)
-        keys = kv_all[:, :, 0].reshape(64 * TOK, D)
         values = jnp.concatenate(
             [kv_all[:, :, 1].reshape(64 * TOK, D), ones[...].reshape(64 * TOK, D)], axis=1
         )
-        scores = lax.dot_general(
-            queries, keys, (((1,), (1,)), ((), ())), preferred_element_type=jnp.float32
-        )
+        scores = jnp.dot(queries, keys_t[...], preferred_element_type=jnp.float32)
         highest = jnp.max(scores, axis=1, keepdims=True)
         weights = jnp.exp2((scores - highest) * (SCALE / math.log(2.0))).astype(jnp.bfloat16)
         total = jnp.dot(weights, values, preferred_element_type=jnp.float32)
@@ -171,22 +169,21 @@
         level = highest * SCALE + jnp.log(weight_sum)
         l_send[y2] = jnp.transpose(level)[0:1, :]
 
-        def send_out(k):
-            z2 = (z + 4 + k) % 8
-            remote(l_send.at[y2], l_recv.at[slot], device(x, y2, z2), 5)
-            remote(o_send.at[y2, z2], o_recv.at[slot], device(x, y2, z2), 4)
-
-        loop(0, 4, send_out)
-        loop(5, 8, send_out)
-        return y2
-
-    def attend_other(step):
-        y2 = attend(step)
-        remote(l_send.at[y2], l_recv.at[slot], device(x, y2, z), 5)
-        remote(o_send.at[y2, z], o_recv.at[slot], device(x, y2, z), 4)
-
-    loop(0, 7, attend_other)
-    attend(7)
+    def send_out(y2, z2):
+        remote(l_send.at[y2], l_recv.at[slot], device(x, y2, z2), 5)
+        remote(o_send.at[y2, z2], o_recv.at[slot], device(x, y2, z2), 4)
+
+    def attend_group(offsets):
+        for k in offsets:
+            attend((y + k) % 8)
+        for k in offsets:
+            y2 = (y + k) % 8
+            loop(1, 8, lambda j: send_out(y2, (z + (j + 3) % 7 + 1) % 8))
+            if k:
+                send_out(y2, z)
+
+    attend_group((4, 5, 3, 6))
+    attend_group((2, 7, 1, 0))
     local(l_send.at[y], l_recv.at[slot], 5)
     local(o_send.at[y, z], o_recv.at[slot], 4)
 
@@ -237,7 +234,7 @@
 
 
 def per_device(query_self, query_cross, key_vectors, values, positions, counts, guidance):
-    anywhere = pl.BlockSpec(memory_space=pl.ANY)
+    anywhere = pl.BlockSpec(memory_space=pltpu.HBM)
     bf16 = jnp.bfloat16
     return pl.pallas_call(
         kernel,
@@ -255,6 +252,7 @@
             pltpu.VMEM((2, 2, 8, TOK, D), bf16),
             pltpu.VMEM((8, 8, TOK, D), bf16),
             pltpu.VMEM((8, 8, TOK, D), bf16),
+            pltpu.VMEM((D, 64 * TOK), bf16),
             pltpu.VMEM((8, 8, TOK, D), bf16),
             pltpu.VMEM((64, TOK, D), bf16),
             pltpu.VMEM((8, 1, D), jnp.float32),

time: 53 us -> 51.9 us (0.979)
  Pallas kernels: 47.3 us -> 46.3 us
    pallas_call x1, Pallas kernels: 47.3 us -> 46.3 us  [per_device(): pl.pallas_call(kernel, out_shape=jax.ShapeDtypeStruct((TOK, HEADS * D //...]
where the time goes in v2:
time: 51.9 us; the launch traced here: 51.6 us
  Pallas kernels  46.3 us (89%)
  local copies, waits for them, and re-layouts  4.64 us (9%)
  between operations  0.68 us (1%)
    pallas_call x1, Pallas kernels, per_device(): pl.pallas_call(kernel, out_shape=jax.ShapeDtypeStruct((TOK, HEADS * D //...  46.3 us
    unnamed x13, local copies, waits for them, and re-layouts  4.64 us

profile of v2, /device:TPU:1, one launch (start us, length us, event | category | flops | bytes accessed | tf_op | source)
XLA Modules:
  0.0 51.6 jit_solution(8679476621175802092)
XLA Ops:
  0.7 0.0 copy-start.4
  0.7 0.0 copy-start.5
  0.7 0.7 %copy-done.4 = s32[256]{0:T(256)S(1)} copy-done((s32[256]{0:T(256)S(1)}, s32[256]{0:T(256)}, u32[]{:S(2)}) %copy-start.4) | copy-done | bytes 1048
  1.3 0.0 copy-done.5
  1.3 0.0 copy-start
  1.3 0.8 %copy-done = bf16[1,16,2048]{2,1,0:T(8,128)(2,1)S(1)} copy-done((bf16[1,16,2048]{2,1,0:T(8,128)(2,1)S(1)}, bf16[1,16,2048]{2,1,0:T(8,128)(2,1)}, u32[]{:S(2)}) %copy-start) | copy-done | bytes 65560
  2.2 0.0 copy-start.1
  2.2 0.8 %copy-done.1 = bf16[1,16,2048]{2,1,0:T(8,128)(2,1)S(1)} copy-done((bf16[1,16,2048]{2,1,0:T(8,128)(2,1)S(1)}, bf16[1,16,2048]{2,1,0:T(8,128)(2,1)}, u32[]{:S(2)}) %copy-start.1) | copy-done | bytes 65560
  3.0 0.0 copy-start.2
  3.0 0.8 %copy-done.2 = bf16[1,16,2048]{2,1,0:T(8,128)(2,1)S(1)} copy-done((bf16[1,16,2048]{2,1,0:T(8,128)(2,1)S(1)}, bf16[1,16,2048]{2,1,0:T(8,128)(2,1)}, u32[]{:S(2)}) %copy-start.2) | copy-done | bytes 65560
  3.9 0.0 copy-start.3
  3.9 0.8 %copy-done.3 = bf16[1,16,2048]{2,1,0:T(8,128)(2,1)S(1)} copy-done((bf16[1,16,2048]{2,1,0:T(8,128)(2,1)S(1)}, bf16[1,16,2048]{2,1,0:T(8,128)(2,1)}, u32[]{:S(2)}) %copy-start.3) | copy-done | bytes 65560
  4.7 46.3 %twin_attention.1 = bf16[16,1024]{1,0:T(8,128)(2,1)S(1)} custom-call(bf16[16,2048]{1,0:T(8,128)(2,1)S(1)} %bitcast.4, bf16[16,2048]{1,0:T(8,128)(2,1)S(1)} %bitcast.5, bf16[16,2048]{1,0:T(8,128)(2,1)S(1)} %bitcast.6, bf16[16,2048]{1,0:T(8,128)(2,1)S(1)} %bitcast.7, s32[16]{0:T(128)S(1)} %copy-done.5, s32[256]{0:T(256)S(1)} %copy-done.4, f32[1]{0:T(128)S(6)} %copy.9.guide_hbm), custom_call_target="tpu_custom_call" | custom-call | tf_op jit(solution)/shard_map/twin_attention/pallas_call | solution.py:239
  51.0 0.6 %copy.10 = bf16[16,1024]{1,0:T(8,128)(2,1)} copy(bf16[16,1024]{1,0:T(8,128)(2,1)S(1)} %twin_attention.1) | data formatting | bytes 65536
Async XLA Ops:
  0.7 0.7 %copy-start.4 = (s32[256]{0:T(256)S(1)}, s32[256]{0:T(256)}, u32[]{:S(2)}) copy-start(s32[256]{0:T(256)} %counts_hbm.1) | copy-start | bytes 3076
  0.7 0.7 %copy-start.5 = (s32[16]{0:T(128)S(1)}, s32[16]{0:T(128)}, u32[]{:S(2)}) copy-start(s32[16]{0:T(128)} %pos_hbm.1) | copy-start | bytes 196
  1.3 0.8 %copy-start = (bf16[1,16,2048]{2,1,0:T(8,128)(2,1)S(1)}, bf16[1,16,2048]{2,1,0:T(8,128)(2,1)}, u32[]{:S(2)}) copy-start(bf16[1,16,2048]{2,1,0:T(8,128)(2,1)} %param.7) | copy-start | bytes 196612
  2.2 0.8 %copy-start.1 = (bf16[1,16,2048]{2,1,0:T(8,128)(2,1)S(1)}, bf16[1,16,2048]{2,1,0:T(8,128)(2,1)}, u32[]{:S(2)}) copy-start(bf16[1,16,2048]{2,1,0:T(8,128)(2,1)} %param.8) | copy-start | bytes 196612
  3.0 0.8 %copy-start.2 = (bf16[1,16,2048]{2,1,0:T(8,128)(2,1)S(1)}, bf16[1,16,2048]{2,1,0:T(8,128)(2,1)}, u32[]{:S(2)}) copy-start(bf16[1,16,2048]{2,1,0:T(8,128)(2,1)} %param.9) | copy-start | bytes 196612
  3.9 0.8 %copy-start.3 = (bf16[1,16,2048]{2,1,0:T(8,128)(2,1)S(1)}, bf16[1,16,2048]{2,1,0:T(8,128)(2,1)}, u32[]{:S(2)}) copy-start(bf16[1,16,2048]{2,1,0:T(8,128)(2,1)} %param.10) | copy-start | bytes 196612

commit v3 on v2

--- a/solution.py
+++ b/solution.py
@@ -31,7 +31,7 @@
     out_ref,
     raw, pos, counts, guide, ones,
     kv_send, kv_all, q_rot, q_z, q_all, keys_t, o_send, o_recv, l_send, l_recv, normed, paired,
-    load_sem, send_sem, recv_sem,
+    load_sem, send_sem, recv_sem, kv_sem, qz_sem, qy_sem,
 ):
     cfg = lax.axis_index("cfg")
     tower = lax.axis_index("tower")
@@ -45,18 +45,18 @@
     def signal(target):
         pl.semaphore_signal(barrier, inc=1, device_id=target, device_id_type=MESH)
 
-    def remote(src, dst, target, stage):
+    def remote(src, dst, target, stage, landed):
         pltpu.make_async_remote_copy(
             src_ref=src, dst_ref=dst,
-            send_sem=send_sem.at[stage], recv_sem=recv_sem.at[stage],
+            send_sem=send_sem.at[stage], recv_sem=landed,
             device_id=target, device_id_type=MESH,
         ).start()
 
-    def local(src, dst, stage):
-        pltpu.make_async_copy(src, dst, recv_sem.at[stage]).start()
-
-    def arrived(like, stage):
-        pltpu.make_async_copy(like, like, recv_sem.at[stage]).wait()
+    def local(src, dst, landed):
+        pltpu.make_async_copy(src, dst, landed).start()
+
+    def arrived(like, landed):
+        pltpu.make_async_copy(like, like, landed).wait()
 
     def sent(like, stage):
         pltpu.make_async_copy(like, like, send_sem.at[stage]).wait()
@@ -115,21 +115,38 @@
 
     own_slot = y * 2 + zl
 
-    def send_kv(k):
-        y2, zl2 = lo_peer(k)
-        remote(kv_send.at[y2 * 2 + zl2], kv_all.at[x, own_slot], device(x, y2, tower * 2 + zl2), 0)
-
     def q_for(z2):
         return q_rot.at[(z // 6 + z2 // 6) % 2, z2 % 2]
 
-    def send_q(k):
-        z2 = (z + k) % 8
-        remote(q_for(z2), q_z.at[z], device(x, y, z2), 1)
-
-    local(kv_send.at[own_slot], kv_all.at[x, own_slot], 0)
-    local(q_for(z), q_z.at[z], 1)
-    loop(1, 16, send_kv)
-    loop(1, 8, send_q)
+    def send_kv(y2, zl2):
+        remote(
+            kv_send.at[y2 * 2 + zl2], kv_all.at[x, own_slot],
+            device(x, y2, tower * 2 + zl2), 0, kv_sem.at[own_slot],
+        )
+
+    def send_q(z2):
+        remote(q_for(z2), q_z.at[z], device(x, y, z2), 1, qz_sem.at[z])
+
+    def pass_kv(block, source):
+        for k in (2, 1, 3):
+            remote(block, kv_all.at[x, source], device((x + k) % 4, y, z), 2, recv_sem.at[2])
+
+    def pass_q(block, source):
+        def pass_one(j):
+            y2 = (y + (j + 3) % 7 + 1) % 8
+            remote(block.at[y2], q_all.at[y, source], device(x, y2, z), 3, qy_sem.at[y])
+
+        loop(0, 7, pass_one)
+        local(block.at[y], q_all.at[y, source], qy_sem.at[y])
+
+    for k in (4, 3, 5, 2, 6, 1, 7):
+        send_kv((y + k) % 8, zl)
+        send_kv((y + k) % 8, 1 - zl)
+        send_q((z + k) % 8)
+    send_kv(y, 1 - zl)
+    local(kv_send.at[own_slot], kv_all.at[x, own_slot], kv_sem.at[own_slot])
+    pass_kv(kv_send.at[own_slot], own_slot)
+    pass_q(q_for(z), z)
 
     def flags(i):
         count = counts[tower * 64 + (i % 2) * 32 + (i // 16) * 8 + (i // 2) % 8]
@@ -137,19 +154,20 @@
 
     loop(0, 64, flags)
 
-    arrived(kv_all.at[x], 0)
-    for k in (2, 1, 3):
-        remote(kv_all.at[x], kv_all.at[x], device((x + k) % 4, y, z), 2)
-    arrived(q_z, 1)
-
-    def pass_q(k):
-        y2 = (y + k) % 8
-        remote(q_z.at[:, y2], q_all.at[y], device(x, y2, z), 3)
-
-    local(q_z.at[:, y], q_all.at[y], 3)
-    loop(1, 8, pass_q)
-    arrived(kv_all.at[pl.ds(0, 3)], 2)
-    arrived(q_all, 3)
+    def kv_from(y2, zl2):
+        source = y2 * 2 + zl2
+        arrived(kv_all.at[x, source], kv_sem.at[source])
+        pass_kv(kv_all.at[x, source], source)
+
+    kv_from(y, 1 - zl)
+    for k in (1, 7, 2, 6, 3, 5, 4):
+        z2 = (z + k) % 8
+        arrived(q_z.at[z2], qz_sem.at[z2])
+        pass_q(q_z.at[z2], z2)
+        kv_from((y + k) % 8, zl)
+        kv_from((y + k) % 8, 1 - zl)
+    arrived(kv_all.at[x, own_slot], kv_sem.at[own_slot])
+    arrived(kv_all.at[pl.ds(0, 3)], recv_sem.at[2])
 
     slot = tower * HEADS + own_slot
 
@@ -170,10 +188,12 @@
         l_send[y2] = jnp.transpose(level)[0:1, :]
 
     def send_out(y2, z2):
-        remote(l_send.at[y2], l_recv.at[slot], device(x, y2, z2), 5)
-        remote(o_send.at[y2, z2], o_recv.at[slot], device(x, y2, z2), 4)
+        remote(l_send.at[y2], l_recv.at[slot], device(x, y2, z2), 5, recv_sem.at[5])
+        remote(o_send.at[y2, z2], o_recv.at[slot], device(x, y2, z2), 4, recv_sem.at[4])
 
     def attend_group(offsets):
+        for k in offsets:
+            arrived(q_all.at[(y + k) % 8], qy_sem.at[(y + k) % 8])
         for k in offsets:
             attend((y + k) % 8)
         for k in offsets:
@@ -182,12 +202,12 @@
             if k:
                 send_out(y2, z)
 
-    attend_group((4, 5, 3, 6))
-    attend_group((2, 7, 1, 0))
-    local(l_send.at[y], l_recv.at[slot], 5)
-    local(o_send.at[y, z], o_recv.at[slot], 4)
-
-    arrived(l_recv, 5)
+    attend_group((0, 1, 7, 2))
+    attend_group((6, 3, 5, 4))
+    local(l_send.at[y], l_recv.at[slot], recv_sem.at[5])
+    local(o_send.at[y, z], o_recv.at[slot], recv_sem.at[4])
+
+    arrived(l_recv, recv_sem.at[5])
     levels = l_recv[...].reshape(64, D)
     levels = jnp.transpose(jnp.concatenate([levels, levels], axis=0))
     mine = jnp.zeros((TOK, D), jnp.float32)
@@ -198,7 +218,7 @@
     shares = [jnp.exp(level - top) for level in per_tower]
     share_sum = shares[0] + shares[1] + shares[2]
     shares = [share / share_sum for share in shares]
-    arrived(o_recv, 4)
+    arrived(o_recv, recv_sem.at[4])
     blocks = []
     squares = jnp.zeros((TOK, D), jnp.float32)
     for h in range(HEADS):
@@ -214,8 +234,8 @@
         normed[h] = (blocks[h] * norm).astype(jnp.bfloat16)
 
     half_heads = HEADS // 2
-    remote(normed.at[pl.ds((1 - cfg) * half_heads, half_heads)], paired, {"cfg": 1 - cfg}, 6)
-    arrived(paired, 6)
+    remote(normed.at[pl.ds((1 - cfg) * half_heads, half_heads)], paired, {"cfg": 1 - cfg}, 6, recv_sem.at[6])
+    arrived(paired, recv_sem.at[6])
     for h in range(half_heads):
         here = normed[cfg * half_heads + h].astype(jnp.float32)
         there = paired[h].astype(jnp.float32)
@@ -262,9 +282,12 @@
             pltpu.SemaphoreType.DMA((7,)),
             pltpu.SemaphoreType.DMA((7,)),
             pltpu.SemaphoreType.DMA((7,)),
+            pltpu.SemaphoreType.DMA((16,)),
+            pltpu.SemaphoreType.DMA((8,)),
+            pltpu.SemaphoreType.DMA((8,)),
         ],
         compiler_params=pltpu.CompilerParams(
-            collective_id=0, has_side_effects=True, vmem_limit_bytes=32 * 1024 * 1024
+            collective_id=0, has_side_effects=True, vmem_limit_bytes=56 * 1024 * 1024
         ),
         name="twin_attention",
     )(query_self[0], query_cross[0], key_vectors[0], values[0], positions, counts, guidance)

time: 51.9 us -> 50.4 us (0.971)
  local copies, waits for them, and re-layouts: 4.64 us -> 1.38 us
  Pallas kernels: 46.3 us -> 48.1 us
    unnamed x13 -> x1, local copies, waits for them, and re-layouts: 4.64 us -> 1.38 us
    pallas_call x1, Pallas kernels: 46.3 us -> 48.1 us  [per_device(): pl.pallas_call(kernel, out_shape=jax.ShapeDtypeStruct((TOK, HEADS * D //...]
where the time goes in v3:
time: 50.4 us; the launch traced here: 50.1 us
  Pallas kernels  48.1 us (95%)
  local copies, waits for them, and re-layouts  1.38 us (3%)
  between operations  0.66 us (1%)
    pallas_call x1, Pallas kernels, per_device(): pl.pallas_call(kernel, out_shape=jax.ShapeDtypeStruct((TOK, HEADS * D //...  48.1 us
    unnamed x1, local copies, waits for them, and re-layouts  1.38 us

profile of v3, /device:TPU:1, one launch (start us, length us, event | category | flops | bytes accessed | tf_op | source)
XLA Modules:
  0.0 50.1 jit_solution(17283927296505411679)
XLA Ops:
  0.7 48.1 %twin_attention.1 = bf16[16,1024]{1,0:T(8,128)(2,1)} custom-call(bf16[16,2048]{1,0:T(8,128)(2,1)} %bitcast.4, bf16[16,2048]{1,0:T(8,128)(2,1)} %bitcast.5, bf16[16,2048]{1,0:T(8,128)(2,1)} %bitcast.6, bf16[16,2048]{1,0:T(8,128)(2,1)} %bitcast.7, s32[16]{0:T(128)} %pos_hbm.1, s32[256]{0:T(256)} %counts_hbm.1, f32[1]{0:T(128)S(6)} %copy.9.guide_hbm), custom_call_target="tpu_custom_call" | custom-call | tf_op jit(solution)/shard_map/twin_attention/pallas_call | solution.py:259
  48.8 1.4 %copy.10 = bf16[16,1024]{1,0:T(8,128)(2,1)} copy(bf16[16,1024]{1,0:T(8,128)(2,1)} %twin_attention.1) | data formatting | bytes 65536

commit v4 on v3

--- a/solution.py
+++ b/solution.py
@@ -11,6 +11,7 @@
 D = 128
 TOK = 16
 SCALE = 1.0 / math.sqrt(D)
+NEAR = (0, 1, 7, 2, 6, 3, 5, 4)
 MESH = pl.DeviceIdType.MESH
 
 
@@ -30,8 +31,8 @@
     qs_hbm, qc_hbm, k_hbm, v_hbm, pos_hbm, counts_hbm, guide_hbm,
     out_ref,
     raw, pos, counts, guide, ones,
-    kv_send, kv_all, q_rot, q_z, q_all, keys_t, o_send, o_recv, l_send, l_recv, normed, paired,
-    load_sem, send_sem, recv_sem, kv_sem, qz_sem, qy_sem,
+    kv_send, kv_all, q_rot, q_y, q_all, keys_t, o_send, o_recv, l_send, l_recv, normed, paired,
+    load_sem, send_sem, recv_sem, kv_sem, qy_sem, qz_sem,
 ):
     cfg = lax.axis_index("cfg")
     tower = lax.axis_index("tower")
@@ -108,15 +109,12 @@
         vals = raw[3, :, h * D:(h + 1) * D]
         kv_send[h, 1] = jnp.where(own_valid, vals.astype(jnp.float32), 0.0).astype(jnp.bfloat16)
     for h in range(HEADS):
-        q_rot[0, h % 2, h // 2] = rope(0, h).astype(jnp.bfloat16)
-        q_rot[1, h % 2, h // 2] = rope(1, h).astype(jnp.bfloat16)
+        q_rot[h // 2, 0, h % 2] = rope(0, h).astype(jnp.bfloat16)
+        q_rot[h // 2, 1, h % 2] = rope(1, h).astype(jnp.bfloat16)
 
     pl.semaphore_wait(barrier, 15 + 7 + 3 + 1)
 
     own_slot = y * 2 + zl
-
-    def q_for(z2):
-        return q_rot.at[(z // 6 + z2 // 6) % 2, z2 % 2]
 
     def send_kv(y2, zl2):
         remote(
@@ -124,29 +122,35 @@
             device(x, y2, tower * 2 + zl2), 0, kv_sem.at[own_slot],
         )
 
-    def send_q(z2):
-        remote(q_for(z2), q_z.at[z], device(x, y, z2), 1, qz_sem.at[z])
+    def send_q(k):
+        place = NEAR.index((8 - k) % 8)
+        remote(q_rot.at[(y + k) % 8], q_y.at[place], device(x, (y + k) % 8, z), 1, qy_sem.at[place])
 
     def pass_kv(block, source):
         for k in (2, 1, 3):
             remote(block, kv_all.at[x, source], device((x + k) % 4, y, z), 2, recv_sem.at[2])
 
-    def pass_q(block, source):
+    def q_for(z2, places):
+        return q_y.at[places, (z // 6 + z2 // 6) % 2, z2 % 2]
+
+    def pass_q(first, count):
+        places = pl.ds(first, count)
+
         def pass_one(j):
-            y2 = (y + (j + 3) % 7 + 1) % 8
-            remote(block.at[y2], q_all.at[y, source], device(x, y2, z), 3, qy_sem.at[y])
+            z2 = (z + (j + 3) % 7 + 1) % 8
+            remote(q_for(z2, places), q_all.at[z, places], device(x, y, z2), 3, qz_sem.at[z])
 
         loop(0, 7, pass_one)
-        local(block.at[y], q_all.at[y, source], qy_sem.at[y])
-
+        local(q_for(z, places), q_all.at[z, places], qz_sem.at[z])
+
+    local(q_rot.at[y], q_y.at[0], qy_sem.at[0])
     for k in (4, 3, 5, 2, 6, 1, 7):
+        send_q(k)
         send_kv((y + k) % 8, zl)
         send_kv((y + k) % 8, 1 - zl)
-        send_q((z + k) % 8)
     send_kv(y, 1 - zl)
     local(kv_send.at[own_slot], kv_all.at[x, own_slot], kv_sem.at[own_slot])
     pass_kv(kv_send.at[own_slot], own_slot)
-    pass_q(q_for(z), z)
 
     def flags(i):
         count = counts[tower * 64 + (i % 2) * 32 + (i // 16) * 8 + (i // 2) % 8]
@@ -160,21 +164,23 @@
         pass_kv(kv_all.at[x, source], source)
 
     kv_from(y, 1 - zl)
-    for k in (1, 7, 2, 6, 3, 5, 4):
-        z2 = (z + k) % 8
-        arrived(q_z.at[z2], qz_sem.at[z2])
-        pass_q(q_z.at[z2], z2)
-        kv_from((y + k) % 8, zl)
-        kv_from((y + k) % 8, 1 - zl)
+    arrived(q_y.at[0], qy_sem.at[0])
+    for place in range(1, 8):
+        arrived(q_y.at[place], qy_sem.at[place])
+        if place == 4:
+            pass_q(0, 5)
+        if place == 7:
+            pass_q(5, 3)
+        kv_from((y + NEAR[place]) % 8, zl)
+        kv_from((y + NEAR[place]) % 8, 1 - zl)
     arrived(kv_all.at[x, own_slot], kv_sem.at[own_slot])
     arrived(kv_all.at[pl.ds(0, 3)], recv_sem.at[2])
 
     slot = tower * HEADS + own_slot
-
     keys_t[...] = jnp.transpose(kv_all[:, :, 0].reshape(64 * TOK, D))
 
-    def attend(y2):
-        queries = q_all[y2].reshape(8 * TOK, D)
+    def attend(z2):
+        queries = q_all[z2].reshape(8 * TOK, D)
         values = jnp.concatenate(
             [kv_all[:, :, 1].reshape(64 * TOK, D), ones[...].reshape(64 * TOK, D)], axis=1
         )
@@ -183,36 +189,39 @@
         weights = jnp.exp2((scores - highest) * (SCALE / math.log(2.0))).astype(jnp.bfloat16)
         total = jnp.dot(weights, values, preferred_element_type=jnp.float32)
         weight_sum = total[:, D:]
-        o_send[y2] = (total[:, :D] / weight_sum).astype(jnp.bfloat16).reshape(8, TOK, D)
+        o_send[z2] = (total[:, :D] / weight_sum).astype(jnp.bfloat16).reshape(8, TOK, D)
         level = highest * SCALE + jnp.log(weight_sum)
-        l_send[y2] = jnp.transpose(level)[0:1, :]
-
-    def send_out(y2, z2):
-        remote(l_send.at[y2], l_recv.at[slot], device(x, y2, z2), 5, recv_sem.at[5])
-        remote(o_send.at[y2, z2], o_recv.at[slot], device(x, y2, z2), 4, recv_sem.at[4])
+        l_send[z2] = jnp.transpose(level)[0:1, :]
+
+    def send_out(z2, place):
+        target = device(x, (y + 8 + ((place + 1) // 2) * (2 * (place % 2) - 1)) % 8, z2)
+        remote(l_send.at[z2], l_recv.at[slot], target, 5, recv_sem.at[5])
+        remote(o_send.at[z2, place], o_recv.at[slot], target, 4, recv_sem.at[4])
 
     def attend_group(offsets):
         for k in offsets:
-            arrived(q_all.at[(y + k) % 8], qy_sem.at[(y + k) % 8])
+            arrived(q_all.at[(z + k) % 8], qz_sem.at[(z + k) % 8])
         for k in offsets:
-            attend((y + k) % 8)
+            attend((z + k) % 8)
         for k in offsets:
-            y2 = (y + k) % 8
-            loop(1, 8, lambda j: send_out(y2, (z + (j + 3) % 7 + 1) % 8))
+            z2 = (z + k) % 8
+            loop(0, 7, lambda j: send_out(z2, 7 - j))
             if k:
-                send_out(y2, z)
+                send_out(z2, 0)
 
     attend_group((0, 1, 7, 2))
     attend_group((6, 3, 5, 4))
-    local(l_send.at[y], l_recv.at[slot], recv_sem.at[5])
-    local(o_send.at[y, z], o_recv.at[slot], recv_sem.at[4])
+    local(l_send.at[z], l_recv.at[slot], recv_sem.at[5])
+    local(o_send.at[z, 0], o_recv.at[slot], recv_sem.at[4])
 
     arrived(l_recv, recv_sem.at[5])
     levels = l_recv[...].reshape(64, D)
     levels = jnp.transpose(jnp.concatenate([levels, levels], axis=0))
+    apart = (y + 8 - lane % HEADS // 2) % 8
+    place = jnp.where(apart <= 4, jnp.maximum(2 * apart - 1, 0), 16 - 2 * apart)
     mine = jnp.zeros((TOK, D), jnp.float32)
-    for z2 in range(8):
-        mine = jnp.where(z == z2, levels[z2 * TOK:(z2 + 1) * TOK], mine)
+    for at in range(8):
+        mine = jnp.where(place == at, levels[at * TOK:(at + 1) * TOK], mine)
     per_tower = [mine[:, t * HEADS:(t + 1) * HEADS] for t in range(3)]
     top = jnp.maximum(jnp.maximum(per_tower[0], per_tower[1]), per_tower[2])
     shares = [jnp.exp(level - top) for level in per_tower]
@@ -245,7 +254,7 @@
         out_ref[:, h * D:(h + 1) * D] = guided.astype(jnp.bfloat16)
 
     sent(kv_send.at[pl.ds(0, 15)], 0)
-    sent(q_z.at[pl.ds(0, 7)], 1)
+    sent(q_y.at[pl.ds(0, 7)], 1)
     sent(kv_all.at[pl.ds(0, 3)], 2)
     sent(q_all.at[pl.ds(0, 7)], 3)
     sent(o_recv.at[pl.ds(0, 63)], 4)
@@ -269,8 +278,8 @@
             pltpu.VMEM((64, TOK, D), bf16),
             pltpu.VMEM((HEADS, 2, TOK, D), bf16),
             pltpu.VMEM((4, HEADS, 2, TOK, D), bf16),
-            pltpu.VMEM((2, 2, 8, TOK, D), bf16),
-            pltpu.VMEM((8, 8, TOK, D), bf16),
+            pltpu.VMEM((8, 2, 2, TOK, D), bf16),
+            pltpu.VMEM((8, 2, 2, TOK, D), bf16),
             pltpu.VMEM((8, 8, TOK, D), bf16),
             pltpu.VMEM((D, 64 * TOK), bf16),
             pltpu.VMEM((8, 8, TOK, D), bf16),

time: 50.4 us -> 48.4 us (0.960)
  Pallas kernels: 48.1 us -> 46.1 us
    pallas_call x1, Pallas kernels: 48.1 us -> 46.1 us  [per_device(): pl.pallas_call(kernel, out_shape=jax.ShapeDtypeStruct((TOK, HEADS * D //...]
where the time goes in v4:
time: 48.4 us; the launch traced here: 48.2 us
  Pallas kernels  46.1 us (95%)
  local copies, waits for them, and re-layouts  1.38 us (3%)
  between operations  0.66 us (1%)
    pallas_call x1, Pallas kernels, per_device(): pl.pallas_call(kernel, out_shape=jax.ShapeDtypeStruct((TOK, HEADS * D //...  46.1 us
    unnamed x1, local copies, waits for them, and re-layouts  1.38 us

profile of v4, /device:TPU:1, one launch (start us, length us, event | category | flops | bytes accessed | tf_op | source)
XLA Modules:
  0.0 48.2 jit_solution(14927044693673215281)
XLA Ops:
  0.7 46.1 %twin_attention.1 = bf16[16,1024]{1,0:T(8,128)(2,1)} custom-call(bf16[16,2048]{1,0:T(8,128)(2,1)} %bitcast.4, bf16[16,2048]{1,0:T(8,128)(2,1)} %bitcast.5, bf16[16,2048]{1,0:T(8,128)(2,1)} %bitcast.6, bf16[16,2048]{1,0:T(8,128)(2,1)} %bitcast.7, s32[16]{0:T(128)} %pos_hbm.1, s32[256]{0:T(256)} %counts_hbm.1, f32[1]{0:T(128)S(6)} %copy.9.guide_hbm), custom_call_target="tpu_custom_call" | custom-call | tf_op jit(solution)/shard_map/twin_attention/pallas_call | solution.py:268
  46.8 1.4 %copy.10 = bf16[16,1024]{1,0:T(8,128)(2,1)} copy(bf16[16,1024]{1,0:T(8,128)(2,1)} %twin_attention.1) | data formatting | bytes 65536

commit v5 on v4

--- a/solution.py
+++ b/solution.py
@@ -28,9 +28,9 @@
 
 
 def kernel(
-    qs_hbm, qc_hbm, k_hbm, v_hbm, pos_hbm, counts_hbm, guide_hbm,
+    qs_hbm, qc_hbm, k_hbm, v_hbm, pos_hbm, counts_hbm,
     out_ref,
-    raw, pos, counts, guide, ones,
+    raw, pos, counts, ones,
     kv_send, kv_all, q_rot, q_y, q_all, keys_t, o_send, o_recv, l_send, l_recv, normed, paired,
     load_sem, send_sem, recv_sem, kv_sem, qy_sem, qz_sem,
 ):
@@ -80,7 +80,6 @@
         pltpu.make_async_copy(v_hbm, raw.at[3], load_sem.at[3]),
         pltpu.make_async_copy(qs_hbm, raw.at[0], load_sem.at[0]),
         pltpu.make_async_copy(qc_hbm, raw.at[1], load_sem.at[1]),
-        pltpu.make_async_copy(guide_hbm, guide, load_sem.at[6]),
     ]
     for copy in loads:
         copy.start()
@@ -126,9 +125,9 @@
         place = NEAR.index((8 - k) % 8)
         remote(q_rot.at[(y + k) % 8], q_y.at[place], device(x, (y + k) % 8, z), 1, qy_sem.at[place])
 
-    def pass_kv(block, source):
+    def pass_kv(pair):
         for k in (2, 1, 3):
-            remote(block, kv_all.at[x, source], device((x + k) % 4, y, z), 2, recv_sem.at[2])
+            remote(pair, pair, device((x + k) % 4, y, z), 2, recv_sem.at[2])
 
     def q_for(z2, places):
         return q_y.at[places, (z // 6 + z2 // 6) % 2, z2 % 2]
@@ -145,12 +144,12 @@
 
     local(q_rot.at[y], q_y.at[0], qy_sem.at[0])
     for k in (4, 3, 5, 2, 6, 1, 7):
-        send_q(k)
         send_kv((y + k) % 8, zl)
         send_kv((y + k) % 8, 1 - zl)
     send_kv(y, 1 - zl)
+    for k in (4, 3, 5, 2, 6, 1, 7):
+        send_q(k)
     local(kv_send.at[own_slot], kv_all.at[x, own_slot], kv_sem.at[own_slot])
-    pass_kv(kv_send.at[own_slot], own_slot)
 
     def flags(i):
         count = counts[tower * 64 + (i % 2) * 32 + (i // 16) * 8 + (i // 2) % 8]
@@ -158,22 +157,19 @@
 
     loop(0, 64, flags)
 
-    def kv_from(y2, zl2):
-        source = y2 * 2 + zl2
-        arrived(kv_all.at[x, source], kv_sem.at[source])
-        pass_kv(kv_all.at[x, source], source)
-
-    kv_from(y, 1 - zl)
+    arrived(kv_all.at[x, own_slot], kv_sem.at[own_slot])
     arrived(q_y.at[0], qy_sem.at[0])
+    for place in range(8):
+        y2 = (y + NEAR[place]) % 8
+        pair = kv_all.at[x, pl.ds(2 * y2, 2)]
+        for zl2 in range(2) if place else ():
+            arrived(kv_all.at[x, 2 * y2 + zl2], kv_sem.at[2 * y2 + zl2])
+        if place == 0:
+            arrived(kv_all.at[x, y * 2 + 1 - zl], kv_sem.at[y * 2 + 1 - zl])
+        pass_kv(pair)
     for place in range(1, 8):
         arrived(q_y.at[place], qy_sem.at[place])
-        if place == 4:
-            pass_q(0, 5)
-        if place == 7:
-            pass_q(5, 3)
-        kv_from((y + NEAR[place]) % 8, zl)
-        kv_from((y + NEAR[place]) % 8, 1 - zl)
-    arrived(kv_all.at[x, own_slot], kv_sem.at[own_slot])
+    pass_q(0, 8)
     arrived(kv_all.at[pl.ds(0, 3)], recv_sem.at[2])
 
     slot = tower * HEADS + own_slot
@@ -209,8 +205,8 @@
             if k:
                 send_out(z2, 0)
 
-    attend_group((0, 1, 7, 2))
-    attend_group((6, 3, 5, 4))
+    attend_group((4, 5, 3, 6))
+    attend_group((2, 7, 1, 0))
     local(l_send.at[z], l_recv.at[slot], recv_sem.at[5])
     local(o_send.at[z, 0], o_recv.at[slot], recv_sem.at[4])
 
@@ -246,12 +242,9 @@
     remote(normed.at[pl.ds((1 - cfg) * half_heads, half_heads)], paired, {"cfg": 1 - cfg}, 6, recv_sem.at[6])
     arrived(paired, recv_sem.at[6])
     for h in range(half_heads):
-        here = normed[cfg * half_heads + h].astype(jnp.float32)
-        there = paired[h].astype(jnp.float32)
-        conditional = jnp.where(cfg == 0, here, there)
-        unconditional = jnp.where(cfg == 0, there, here)
-        guided = unconditional + guide[0] * (conditional - unconditional)
-        out_ref[:, h * D:(h + 1) * D] = guided.astype(jnp.bfloat16)
+        here = normed[cfg * half_heads + h]
+        out_ref[cfg, :, h * D:(h + 1) * D] = here
+        out_ref[1 - cfg, :, h * D:(h + 1) * D] = paired[h]
 
     sent(kv_send.at[pl.ds(0, 15)], 0)
     sent(q_y.at[pl.ds(0, 7)], 1)
@@ -265,16 +258,15 @@
 def per_device(query_self, query_cross, key_vectors, values, positions, counts, guidance):
     anywhere = pl.BlockSpec(memory_space=pltpu.HBM)
     bf16 = jnp.bfloat16
-    return pl.pallas_call(
+    both = pl.pallas_call(
         kernel,
-        out_shape=jax.ShapeDtypeStruct((TOK, HEADS * D // 2), bf16),
-        in_specs=[anywhere] * 7,
+        out_shape=jax.ShapeDtypeStruct((2, TOK, HEADS * D // 2), bf16),
+        in_specs=[anywhere] * 6,
         out_specs=pl.BlockSpec(memory_space=pltpu.VMEM),
         scratch_shapes=[
             pltpu.VMEM((4, TOK, HEADS * D), bf16),
             pltpu.SMEM((TOK,), jnp.int32),
             pltpu.SMEM((256,), jnp.int32),
-            pltpu.SMEM((1,), jnp.float32),
             pltpu.VMEM((64, TOK, D), bf16),
             pltpu.VMEM((HEADS, 2, TOK, D), bf16),
             pltpu.VMEM((4, HEADS, 2, TOK, D), bf16),
@@ -299,7 +291,10 @@
             collective_id=0, has_side_effects=True, vmem_limit_bytes=56 * 1024 * 1024
         ),
         name="twin_attention",
-    )(query_self[0], query_cross[0], key_vectors[0], values[0], positions, counts, guidance)
+    )(query_self[0], query_cross[0], key_vectors[0], values[0], positions, counts)
+    conditional = both[0].astype(jnp.float32)
+    unconditional = both[1].astype(jnp.float32)
+    return (unconditional + guidance * (conditional - unconditional)).astype(bf16)
 
 
 def solution(mesh):

time: 48.4 us -> 46.2 us (0.955)
  Pallas kernels: 46.1 us -> 43.9 us
  other arithmetic: 0 us -> 1.41 us
  local copies, waits for them, and re-layouts: 1.38 us -> 0 us
    pallas_call x1, Pallas kernels: 46.1 us -> 43.9 us  [per_device(): pl.pallas_call(kernel, out_shape=jax.ShapeDtypeStruct((2, TOK, HEADS * D...]
    convert_element_type x0 -> x1, other arithmetic: none -> 1.41 us  [per_device(): (unconditional + guidance * (conditional - unconditional)).astype(bf16)]
    unnamed x1 -> x0, local copies, waits for them, and re-layouts: 1.38 us -> none
where the time goes in v5:
time: 46.2 us; the launch traced here: 45.9 us
  Pallas kernels  43.9 us (95%)
  other arithmetic  1.41 us (3%)
  between operations  0.66 us (1%)
    pallas_call x1, Pallas kernels, per_device(): pl.pallas_call(kernel, out_shape=jax.ShapeDtypeStruct((2, TOK, HEADS * D...  43.9 us
    convert_element_type x1, other arithmetic, per_device(): (unconditional + guidance * (conditional - unconditional)).astype(bf16)  1.41 us

profile of v5, /device:TPU:1, one launch (start us, length us, event | category | flops | bytes accessed | tf_op | source)
XLA Modules:
  0.0 45.9 jit_solution(11947058896096681385)
XLA Ops:
  0.7 43.9 %twin_attention.1 = bf16[2,16,1024]{2,1,0:T(8,128)(2,1)} custom-call(bf16[16,2048]{1,0:T(8,128)(2,1)} %bitcast.12, bf16[16,2048]{1,0:T(8,128)(2,1)} %bitcast.13, bf16[16,2048]{1,0:T(8,128)(2,1)} %bitcast.14, bf16[16,2048]{1,0:T(8,128)(2,1)} %bitcast.15, s32[16]{0:T(128)} %pos_hbm.1, s32[256]{0:T(256)} %counts_hbm.1), custom_call_target="tpu_custom_call" | custom-call | tf_op jit(solution)/shard_map/twin_attention/pallas_call | solution.py:261
  44.5 1.4 %fusion.1 = bf16[16,1024]{1,0:T(8,128)(2,1)} fusion(bf16[2,16,1024]{2,1,0:T(8,128)(2,1)} %twin_attention.1, f32[]{:T(128)} %bitcast.11), kind=kLoop, calls=%fused_computation.3 | loop fusion | flops 98304 | bytes 98308 | tf_op jit(solution)/shard_map/convert_element_type | solution.py:297

commit v6 on v5

--- a/solution.py
+++ b/solution.py
@@ -40,9 +40,6 @@
     zl, x, y = seq // 32, (seq // 8) % 4, seq % 8
     z = tower * 2 + zl
 
-    def lo_peer(k):
-        return (y + k // 2) % 8, (zl + k % 2) % 2
-
     def signal(target):
         pl.semaphore_signal(barrier, inc=1, device_id=target, device_id_type=MESH)
 
@@ -64,13 +61,13 @@
 
     barrier = pltpu.get_barrier_semaphore()
 
-    def greet_lo(k):
-        y2, zl2 = lo_peer(k)
-        signal(device(x, y2, tower * 2 + zl2))
-
-    loop(1, 16, greet_lo)
-    loop(1, 8, lambda k: signal(device(x, y, (z + k) % 8)))
-    loop(1, 4, lambda k: signal(device((x + k) % 4, y, z)))
+    for k in (4, 3, 5, 2, 6, 1, 7):
+        signal(device(x, (y + k) % 8, tower * 2 + 1 - zl))
+    for k in (4, 3, 5, 2, 6, 1, 7):
+        signal(device(x, (y + k) % 8, z))
+        signal(device(x, y, (z + k) % 8))
+    for k in (2, 1, 3):
+        signal(device((x + k) % 4, y, z))
     signal({"cfg": 1 - cfg})
 
     loads = [
@@ -111,7 +108,7 @@
         q_rot[h // 2, 0, h % 2] = rope(0, h).astype(jnp.bfloat16)
         q_rot[h // 2, 1, h % 2] = rope(1, h).astype(jnp.bfloat16)
 
-    pl.semaphore_wait(barrier, 15 + 7 + 3 + 1)
+    pl.semaphore_wait(barrier, 7 + 7 + 7 + 3 + 1)
 
     own_slot = y * 2 + zl
 
@@ -135,11 +132,10 @@
     def pass_q(first, count):
         places = pl.ds(first, count)
 
-        def pass_one(j):
-            z2 = (z + (j + 3) % 7 + 1) % 8
+        for k in (4, 3, 5, 2, 6, 1, 7):
+            z2 = (z + k) % 8
             remote(q_for(z2, places), q_all.at[z, places], device(x, y, z2), 3, qz_sem.at[z])
 
-        loop(0, 7, pass_one)
         local(q_for(z, places), q_all.at[z, places], qz_sem.at[z])
 
     local(q_rot.at[y], q_y.at[0], qy_sem.at[0])
@@ -154,8 +150,6 @@
     def flags(i):
         count = counts[tower * 64 + (i % 2) * 32 + (i // 16) * 8 + (i // 2) % 8]
         ones[i] = jnp.where(row < count, 1.0, 0.0).astype(jnp.bfloat16)
-
-    loop(0, 64, flags)
 
     arrived(kv_all.at[x, own_slot], kv_sem.at[own_slot])
     arrived(q_y.at[0], qy_sem.at[0])
@@ -170,6 +164,7 @@
     for place in range(1, 8):
         arrived(q_y.at[place], qy_sem.at[place])
     pass_q(0, 8)
+    loop(0, 64, flags)
     arrived(kv_all.at[pl.ds(0, 3)], recv_sem.at[2])
 
     slot = tower * HEADS + own_slot
@@ -190,7 +185,7 @@
         l_send[z2] = jnp.transpose(level)[0:1, :]
 
     def send_out(z2, place):
-        target = device(x, (y + 8 + ((place + 1) // 2) * (2 * (place % 2) - 1)) % 8, z2)
+        target = device(x, (y + NEAR[place]) % 8, z2)
         remote(l_send.at[z2], l_recv.at[slot], target, 5, recv_sem.at[5])
         remote(o_send.at[z2, place], o_recv.at[slot], target, 4, recv_sem.at[4])
 
@@ -201,9 +196,8 @@
             attend((z + k) % 8)
         for k in offsets:
             z2 = (z + k) % 8
-            loop(0, 7, lambda j: send_out(z2, 7 - j))
-            if k:
-                send_out(z2, 0)
+            for place in range(7, -1 if k else 0, -1):
+                send_out(z2, place)
 
     attend_group((4, 5, 3, 6))
     attend_group((2, 7, 1, 0))

time: 46.2 us -> 44.2 us (0.957)
  Pallas kernels: 43.9 us -> 41.9 us
    pallas_call x1, Pallas kernels: 43.9 us -> 41.9 us  [per_device(): pl.pallas_call(kernel, out_shape=jax.ShapeDtypeStruct((2, TOK, HEADS * D...]
where the time goes in v6:
time: 44.2 us; the launch traced here: 44 us
  Pallas kernels  41.9 us (95%)
  other arithmetic  1.41 us (3%)
  between operations  0.66 us (1%)
    pallas_call x1, Pallas kernels, per_device(): pl.pallas_call(kernel, out_shape=jax.ShapeDtypeStruct((2, TOK, HEADS * D...  41.9 us
    convert_element_type x1, other arithmetic, per_device(): (unconditional + guidance * (conditional - unconditional)).astype(bf16)  1.41 us

profile of v6, /device:TPU:1, one launch (start us, length us, event | category | flops | bytes accessed | tf_op | source)
XLA Modules:
  0.0 44.0 jit_solution(7302373717270253073)
XLA Ops:
  0.7 41.9 %twin_attention.1 = bf16[2,16,1024]{2,1,0:T(8,128)(2,1)} custom-call(bf16[16,2048]{1,0:T(8,128)(2,1)} %bitcast.12, bf16[16,2048]{1,0:T(8,128)(2,1)} %bitcast.13, bf16[16,2048]{1,0:T(8,128)(2,1)} %bitcast.14, bf16[16,2048]{1,0:T(8,128)(2,1)} %bitcast.15, s32[16]{0:T(128)} %pos_hbm.1, s32[256]{0:T(256)} %counts_hbm.1), custom_call_target="tpu_custom_call" | custom-call | tf_op jit(solution)/shard_map/twin_attention/pallas_call | solution.py:255
  42.6 1.4 %fusion.1 = bf16[16,1024]{1,0:T(8,128)(2,1)} fusion(bf16[2,16,1024]{2,1,0:T(8,128)(2,1)} %twin_attention.1, f32[]{:T(128)} %bitcast.11), kind=kLoop, calls=%fused_computation.3 | loop fusion | flops 98304 | bytes 98308 | tf_op jit(solution)/shard_map/convert_element_type | solution.py:291

commit v7 on v6

--- a/solution.py
+++ b/solution.py
@@ -28,7 +28,7 @@
 
 
 def kernel(
-    qs_hbm, qc_hbm, k_hbm, v_hbm, pos_hbm, counts_hbm,
+    qs_hbm, qc_hbm, k_hbm, v_hbm, pos_hbm, counts_hbm, guide_ref,
     out_ref,
     raw, pos, counts, ones,
     kv_send, kv_all, q_rot, q_y, q_all, keys_t, o_send, o_recv, l_send, l_recv, normed, paired,
@@ -236,9 +236,12 @@
     remote(normed.at[pl.ds((1 - cfg) * half_heads, half_heads)], paired, {"cfg": 1 - cfg}, 6, recv_sem.at[6])
     arrived(paired, recv_sem.at[6])
     for h in range(half_heads):
-        here = normed[cfg * half_heads + h]
-        out_ref[cfg, :, h * D:(h + 1) * D] = here
-        out_ref[1 - cfg, :, h * D:(h + 1) * D] = paired[h]
+        here = normed[cfg * half_heads + h].astype(jnp.float32)
+        there = paired[h].astype(jnp.float32)
+        conditional = jnp.where(cfg == 0, here, there)
+        unconditional = jnp.where(cfg == 0, there, here)
+        guided = unconditional + guide_ref[0] * (conditional - unconditional)
+        out_ref[:, h * D:(h + 1) * D] = guided.astype(jnp.bfloat16)
 
     sent(kv_send.at[pl.ds(0, 15)], 0)
     sent(q_y.at[pl.ds(0, 7)], 1)
@@ -252,10 +255,10 @@
 def per_device(query_self, query_cross, key_vectors, values, positions, counts, guidance):
     anywhere = pl.BlockSpec(memory_space=pltpu.HBM)
     bf16 = jnp.bfloat16
-    both = pl.pallas_call(
+    return pl.pallas_call(
         kernel,
-        out_shape=jax.ShapeDtypeStruct((2, TOK, HEADS * D // 2), bf16),
-        in_specs=[anywhere] * 6,
+        out_shape=pltpu.VMEM((TOK, HEADS * D // 2), bf16),
+        in_specs=[anywhere] * 6 + [pl.BlockSpec(memory_space=pltpu.SMEM)],
         out_specs=pl.BlockSpec(memory_space=pltpu.VMEM),
         scratch_shapes=[
             pltpu.VMEM((4, TOK, HEADS * D), bf16),
@@ -285,10 +288,7 @@
             collective_id=0, has_side_effects=True, vmem_limit_bytes=56 * 1024 * 1024
         ),
         name="twin_attention",
-    )(query_self[0], query_cross[0], key_vectors[0], values[0], positions, counts)
-    conditional = both[0].astype(jnp.float32)
-    unconditional = both[1].astype(jnp.float32)
-    return (unconditional + guidance * (conditional - unconditional)).astype(bf16)
+    )(query_self[0], query_cross[0], key_vectors[0], values[0], positions, counts, guidance)
 
 
 def solution(mesh):

time: 44.2 us -> 42.8 us (0.968)
  other arithmetic: 1.41 us -> 0 us
  local copies, waits for them, and re-layouts: 0 us -> 0.62 us
  Pallas kernels: 41.9 us -> 41.3 us
    convert_element_type x1 -> x0, other arithmetic: 1.41 us -> none  [per_device(): (unconditional + guidance * (conditional - unconditional)).astype(bf16)]
    unnamed x0 -> x1, local copies, waits for them, and re-layouts: none -> 0.62 us
    pallas_call x1, Pallas kernels: 41.9 us -> 41.3 us  [per_device(): pl.pallas_call(kernel, out_shape=pltpu.VMEM((TOK, HEADS * D // 2), bf16),...]
where the time goes in v7:
time: 42.8 us; the launch traced here: 42.6 us
  Pallas kernels  41.3 us (96%)
  between operations  0.66 us (2%)
  local copies, waits for them, and re-layouts  0.62 us (1%)
    pallas_call x1, Pallas kernels, per_device(): pl.pallas_call(kernel, out_shape=pltpu.VMEM((TOK, HEADS * D // 2), bf16),...  41.3 us

profile of v7, /device:TPU:1, one launch (start us, length us, event | category | flops | bytes accessed | tf_op | source)
XLA Modules:
  0.0 42.6 jit_solution(18222696614911875670)
XLA Ops:
  0.7 41.3 %twin_attention.1 = bf16[16,1024]{1,0:T(8,128)(2,1)S(1)} custom-call(bf16[16,2048]{1,0:T(8,128)(2,1)} %bitcast.4, bf16[16,2048]{1,0:T(8,128)(2,1)} %bitcast.5, bf16[16,2048]{1,0:T(8,128)(2,1)} %bitcast.6, bf16[16,2048]{1,0:T(8,128)(2,1)} %bitcast.7, s32[16]{0:T(128)} %pos_hbm.1, s32[256]{0:T(256)} %counts_hbm.1, f32[1]{0:T(128)S(6)} %copy.10.guide_ref), custom_call_target="tpu_custom_call" | custom-call | tf_op jit(solution)/shard_map/twin_attention/pallas_call | solution.py:258
  42.0 0.6 %copy.9 = bf16[16,1024]{1,0:T(8,128)(2,1)} copy(bf16[16,1024]{1,0:T(8,128)(2,1)S(1)} %twin_attention.1) | data formatting | bytes 65536

commit v8 on v7

--- a/solution.py
+++ b/solution.py
@@ -15,6 +15,19 @@
 MESH = pl.DeviceIdType.MESH
 
 
+def hops(dy, dz):
+    return min(dy, 8 - dy) + min(dz, 8 - dz)
+
+
+AROUND = sorted(
+    ((dy, dz) for dy in range(8) for dz in range(8) if dy or dz), key=lambda d: (-hops(*d), d)
+)
+CLOSE = [d for d in AROUND if hops(*d) <= 5]
+FAR = [d for d in AROUND if hops(*d) > 5]
+FAR_DY = (2, 6, 3, 5, 4)
+FAR_DZ = {dy: [dz for dy2, dz in FAR if dy2 == dy] for dy in FAR_DY}
+
+
 def loop(lo, hi, fn):
     def body(k, carry):
         fn(k)
@@ -31,7 +44,7 @@
     qs_hbm, qc_hbm, k_hbm, v_hbm, pos_hbm, counts_hbm, guide_ref,
     out_ref,
     raw, pos, counts, ones,
-    kv_send, kv_all, q_rot, q_y, q_all, keys_t, o_send, o_recv, l_send, l_recv, normed, paired,
+    kv_send, kv_all, q_rot, q_far, q_all, keys_t, o_send, o_recv, l_send, l_recv, normed, paired,
     load_sem, send_sem, recv_sem, kv_sem, qy_sem, qz_sem,
 ):
     cfg = lax.axis_index("cfg")
@@ -61,11 +74,8 @@
 
     barrier = pltpu.get_barrier_semaphore()
 
-    for k in (4, 3, 5, 2, 6, 1, 7):
-        signal(device(x, (y + k) % 8, tower * 2 + 1 - zl))
-    for k in (4, 3, 5, 2, 6, 1, 7):
-        signal(device(x, (y + k) % 8, z))
-        signal(device(x, y, (z + k) % 8))
+    for dy, dz in CLOSE:
+        signal(device(x, (y + dy) % 8, (z + dz) % 8))
     for k in (2, 1, 3):
         signal(device((x + k) % 4, y, z))
     signal({"cfg": 1 - cfg})
@@ -108,7 +118,7 @@
         q_rot[h // 2, 0, h % 2] = rope(0, h).astype(jnp.bfloat16)
         q_rot[h // 2, 1, h % 2] = rope(1, h).astype(jnp.bfloat16)
 
-    pl.semaphore_wait(barrier, 7 + 7 + 7 + 3 + 1)
+    pl.semaphore_wait(barrier, len(CLOSE) + 3 + 1)
 
     own_slot = y * 2 + zl
 
@@ -118,33 +128,39 @@
             device(x, y2, tower * 2 + zl2), 0, kv_sem.at[own_slot],
         )
 
-    def send_q(k):
-        place = NEAR.index((8 - k) % 8)
-        remote(q_rot.at[(y + k) % 8], q_y.at[place], device(x, (y + k) % 8, z), 1, qy_sem.at[place])
+    def q_for(dy, z2):
+        return q_rot.at[(y + dy) % 8, (z // 6 + z2 // 6) % 2, z2 % 2]
+
+    def place_from(dy):
+        return NEAR.index((8 - dy) % 8)
+
+    def send_q(dy, dz):
+        z2 = (z + dz) % 8
+        block, target = q_all.at[z, place_from(dy)], device(x, (y + dy) % 8, z2)
+        remote(q_for(dy, z2), block, target, 3, qz_sem.at[z])
+
+    def send_far_q(dy, dz):
+        block = q_far.at[FAR.index((dy, dz))]
+        remote(q_for(dy, (z + dz) % 8), block, device(x, (y + dy) % 8, z), 1, qy_sem.at[dy])
+
+    def pass_far_q(dy, dz):
+        block = q_far.at[FAR.index((dy, dz))]
+        target = device(x, y, (z + dz) % 8)
+        remote(block, q_all.at[z, place_from(dy)], target, 3, qz_sem.at[z])
 
     def pass_kv(pair):
         for k in (2, 1, 3):
             remote(pair, pair, device((x + k) % 4, y, z), 2, recv_sem.at[2])
 
-    def q_for(z2, places):
-        return q_y.at[places, (z // 6 + z2 // 6) % 2, z2 % 2]
-
-    def pass_q(first, count):
-        places = pl.ds(first, count)
-
-        for k in (4, 3, 5, 2, 6, 1, 7):
-            z2 = (z + k) % 8
-            remote(q_for(z2, places), q_all.at[z, places], device(x, y, z2), 3, qz_sem.at[z])
-
-        local(q_for(z, places), q_all.at[z, places], qz_sem.at[z])
-
-    local(q_rot.at[y], q_y.at[0], qy_sem.at[0])
     for k in (4, 3, 5, 2, 6, 1, 7):
         send_kv((y + k) % 8, zl)
         send_kv((y + k) % 8, 1 - zl)
     send_kv(y, 1 - zl)
-    for k in (4, 3, 5, 2, 6, 1, 7):
-        send_q(k)
+    for dy, dz in FAR:
+        send_far_q(dy, dz)
+    for dy, dz in CLOSE:
+        send_q(dy, dz)
+    local(q_for(0, z), q_all.at[z, 0], qz_sem.at[z])
     local(kv_send.at[own_slot], kv_all.at[x, own_slot], kv_sem.at[own_slot])
 
     def flags(i):
@@ -152,7 +168,6 @@
         ones[i] = jnp.where(row < count, 1.0, 0.0).astype(jnp.bfloat16)
 
     arrived(kv_all.at[x, own_slot], kv_sem.at[own_slot])
-    arrived(q_y.at[0], qy_sem.at[0])
     for place in range(8):
         y2 = (y + NEAR[place]) % 8
         pair = kv_all.at[x, pl.ds(2 * y2, 2)]
@@ -161,9 +176,10 @@
         if place == 0:
             arrived(kv_all.at[x, y * 2 + 1 - zl], kv_sem.at[y * 2 + 1 - zl])
         pass_kv(pair)
-    for place in range(1, 8):
-        arrived(q_y.at[place], qy_sem.at[place])
-    pass_q(0, 8)
+    for dy in FAR_DY:
+        arrived(q_far.at[pl.ds(0, len(FAR_DZ[dy]))], qy_sem.at[dy])
+        for dz in FAR_DZ[dy]:
+            pass_far_q(dy, dz)
     loop(0, 64, flags)
     arrived(kv_all.at[pl.ds(0, 3)], recv_sem.at[2])
 
@@ -244,9 +260,9 @@
         out_ref[:, h * D:(h + 1) * D] = guided.astype(jnp.bfloat16)
 
     sent(kv_send.at[pl.ds(0, 15)], 0)
-    sent(q_y.at[pl.ds(0, 7)], 1)
+    sent(q_far, 1)
     sent(kv_all.at[pl.ds(0, 3)], 2)
-    sent(q_all.at[pl.ds(0, 7)], 3)
+    sent(o_recv.at[pl.ds(0, 63)], 3)
     sent(o_recv.at[pl.ds(0, 63)], 4)
     sent(l_recv.at[pl.ds(0, 63)], 5)
     sent(paired, 6)
@@ -268,7 +284,7 @@
             pltpu.VMEM((HEADS, 2, TOK, D), bf16),
             pltpu.VMEM((4, HEADS, 2, TOK, D), bf16),
             pltpu.VMEM((8, 2, 2, TOK, D), bf16),
-            pltpu.VMEM((8, 2, 2, TOK, D), bf16),
+            pltpu.VMEM((len(FAR), TOK, D), bf16),
             pltpu.VMEM((8, 8, TOK, D), bf16),
             pltpu.VMEM((D, 64 * TOK), bf16),
             pltpu.VMEM((8, 8, TOK, D), bf16),

time: 42.8 us -> 43.2 us (level)
  no operation moved by 1% of the time
where the time goes in v8:
time: 43.2 us; the launch traced here: 43 us
  Pallas kernels  41.7 us (97%)
  between operations  0.66 us (2%)
  local copies, waits for them, and re-layouts  0.62 us (1%)
    pallas_call x1, Pallas kernels, per_device(): pl.pallas_call(kernel, out_shape=pltpu.VMEM((TOK, HEADS * D // 2), bf16),...  41.7 us

profile of v8, /device:TPU:1, one launch (start us, length us, event | category | flops | bytes accessed | tf_op | source)
XLA Modules:
  0.0 43.0 jit_solution(1852559341677683927)
XLA Ops:
  0.7 41.7 %twin_attention.1 = bf16[16,1024]{1,0:T(8,128)(2,1)S(1)} custom-call(bf16[16,2048]{1,0:T(8,128)(2,1)} %bitcast.4, bf16[16,2048]{1,0:T(8,128)(2,1)} %bitcast.5, bf16[16,2048]{1,0:T(8,128)(2,1)} %bitcast.6, bf16[16,2048]{1,0:T(8,128)(2,1)} %bitcast.7, s32[16]{0:T(128)} %pos_hbm.1, s32[256]{0:T(256)} %counts_hbm.1, f32[1]{0:T(128)S(6)} %copy.10.guide_ref), custom_call_target="tpu_custom_call" | custom-call | tf_op jit(solution)/shard_map/twin_attention/pallas_call | solution.py:274
  42.4 0.6 %copy.9 = bf16[16,1024]{1,0:T(8,128)(2,1)} copy(bf16[16,1024]{1,0:T(8,128)(2,1)S(1)} %twin_attention.1) | data formatting | bytes 65536

commit v9 on v8

--- a/solution.py
+++ b/solution.py
@@ -44,7 +44,7 @@
     qs_hbm, qc_hbm, k_hbm, v_hbm, pos_hbm, counts_hbm, guide_ref,
     out_ref,
     raw, pos, counts, ones,
-    kv_send, kv_all, q_rot, q_far, q_all, keys_t, o_send, o_recv, l_send, l_recv, normed, paired,
+    kv_send, kv_all, q_rot, q_far, q_all, keys_t, o_send, o_recv, l_send, l_recv, merged, paired, scale_here, scale_there,
     load_sem, send_sem, recv_sem, kv_sem, qy_sem, qz_sem,
 ):
     cfg = lax.axis_index("cfg")
@@ -71,14 +71,6 @@
 
     def sent(like, stage):
         pltpu.make_async_copy(like, like, send_sem.at[stage]).wait()
-
-    barrier = pltpu.get_barrier_semaphore()
-
-    for dy, dz in CLOSE:
-        signal(device(x, (y + dy) % 8, (z + dz) % 8))
-    for k in (2, 1, 3):
-        signal(device((x + k) % 4, y, z))
-    signal({"cfg": 1 - cfg})
 
     loads = [
         pltpu.make_async_copy(pos_hbm, pos, load_sem.at[4]),
@@ -90,6 +82,15 @@
     ]
     for copy in loads:
         copy.start()
+
+    barrier = pltpu.get_barrier_semaphore()
+
+    for dy, dz in CLOSE:
+        signal(device(x, (y + dy) % 8, (z + dz) % 8))
+    for k in (2, 1, 3):
+        signal(device((x + k) % 4, y, z))
+    signal({"cfg": 1 - cfg})
+
     for copy in loads:
         copy.wait()
 
@@ -215,8 +216,10 @@
             for place in range(7, -1 if k else 0, -1):
                 send_out(z2, place)
 
-    attend_group((4, 5, 3, 6))
-    attend_group((2, 7, 1, 0))
+    attend_group((4,))
+    attend_group((5, 3))
+    attend_group((6, 2))
+    attend_group((7, 1, 0))
     local(l_send.at[z], l_recv.at[slot], recv_sem.at[5])
     local(o_send.at[z, 0], o_recv.at[slot], recv_sem.at[4])
 
@@ -234,28 +237,37 @@
     share_sum = shares[0] + shares[1] + shares[2]
     shares = [share / share_sum for share in shares]
     arrived(o_recv, recv_sem.at[4])
-    blocks = []
     squares = jnp.zeros((TOK, D), jnp.float32)
     for h in range(HEADS):
         block = o_recv[3 * HEADS + h].astype(jnp.float32)
         for t in range(3):
             block += shares[t][:, h:h + 1] * o_recv[t * HEADS + h].astype(jnp.float32)
-        block = jnp.where(own_valid, block, 0.0).astype(jnp.bfloat16).astype(jnp.float32)
-        blocks.append(block)
+        block = jnp.where(own_valid, block, 0.0).astype(jnp.bfloat16)
+        merged[h] = block
+        block = block.astype(jnp.float32)
         squares += block * block
+
+    half_heads = HEADS // 2
+    remote(
+        merged.at[pl.ds((1 - cfg) * half_heads, half_heads)], paired,
+        {"cfg": 1 - cfg}, 6, recv_sem.at[6],
+    )
     mean = jnp.sum(squares, axis=1, keepdims=True) * (1.0 / (HEADS * D))
-    norm = lax.rsqrt(mean + 1e-06)
-    for h in range(HEADS):
-        normed[h] = (blocks[h] * norm).astype(jnp.bfloat16)
-
-    half_heads = HEADS // 2
-    remote(normed.at[pl.ds((1 - cfg) * half_heads, half_heads)], paired, {"cfg": 1 - cfg}, 6, recv_sem.at[6])
+    scale_here[...] = jnp.broadcast_to(lax.rsqrt(mean + 1e-06), (TOK, D))
+    remote(scale_here, scale_there, {"cfg": 1 - cfg}, 7, recv_sem.at[7])
+
+    def rounded(block, scale):
+        return (block.astype(jnp.float32) * scale).astype(jnp.bfloat16).astype(jnp.float32)
+
+    own_half = [
+        rounded(merged[cfg * half_heads + h], scale_here[...]) for h in range(half_heads)
+    ]
     arrived(paired, recv_sem.at[6])
+    arrived(scale_there, recv_sem.at[7])
     for h in range(half_heads):
-        here = normed[cfg * half_heads + h].astype(jnp.float32)
-        there = paired[h].astype(jnp.float32)
-        conditional = jnp.where(cfg == 0, here, there)
-        unconditional = jnp.where(cfg == 0, there, here)
+        there = rounded(paired[h], scale_there[...])
+        conditional = jnp.where(cfg == 0, own_half[h], there)
+        unconditional = jnp.where(cfg == 0, there, own_half[h])
         guided = unconditional + guide_ref[0] * (conditional - unconditional)
         out_ref[:, h * D:(h + 1) * D] = guided.astype(jnp.bfloat16)
 
@@ -266,6 +278,7 @@
     sent(o_recv.at[pl.ds(0, 63)], 4)
     sent(l_recv.at[pl.ds(0, 63)], 5)
     sent(paired, 6)
+    sent(scale_there, 7)
 
 
 def per_device(query_self, query_cross, key_vectors, values, positions, counts, guidance):
@@ -293,9 +306,11 @@
             pltpu.VMEM((64, 1, D), jnp.float32),
             pltpu.VMEM((HEADS, TOK, D), bf16),
             pltpu.VMEM((HEADS // 2, TOK, D), bf16),
-            pltpu.SemaphoreType.DMA((7,)),
-            pltpu.SemaphoreType.DMA((7,)),
-            pltpu.SemaphoreType.DMA((7,)),
+            pltpu.VMEM((TOK, D), jnp.float32),
+            pltpu.VMEM((TOK, D), jnp.float32),
+            pltpu.SemaphoreType.DMA((6,)),
+            pltpu.SemaphoreType.DMA((8,)),
+            pltpu.SemaphoreType.DMA((8,)),
             pltpu.SemaphoreType.DMA((16,)),
             pltpu.SemaphoreType.DMA((8,)),
             pltpu.SemaphoreType.DMA((8,)),

time: 43.2 us -> 42.5 us (0.984)
  Pallas kernels: 41.7 us -> 41.1 us
    pallas_call x1, Pallas kernels: 41.7 us -> 41.1 us  [per_device(): pl.pallas_call(kernel, out_shape=pltpu.VMEM((TOK, HEADS * D // 2), bf16),...]
where the time goes in v9:
time: 42.5 us; the launch traced here: 42.4 us
  Pallas kernels  41.1 us (97%)
  between operations  0.66 us (2%)
  local copies, waits for them, and re-layouts  0.62 us (1%)
    pallas_call x1, Pallas kernels, per_device(): pl.pallas_call(kernel, out_shape=pltpu.VMEM((TOK, HEADS * D // 2), bf16),...  41.1 us

profile of v9, /device:TPU:1, one launch (start us, length us, event | category | flops | bytes accessed | tf_op | source)
XLA Modules:
  0.0 42.4 jit_solution(3282610888543970178)
XLA Ops:
  0.7 41.1 %twin_attention.1 = bf16[16,1024]{1,0:T(8,128)(2,1)S(1)} custom-call(bf16[16,2048]{1,0:T(8,128)(2,1)} %bitcast.4, bf16[16,2048]{1,0:T(8,128)(2,1)} %bitcast.5, bf16[16,2048]{1,0:T(8,128)(2,1)} %bitcast.6, bf16[16,2048]{1,0:T(8,128)(2,1)} %bitcast.7, s32[16]{0:T(128)} %pos_hbm.1, s32[256]{0:T(256)} %counts_hbm.1, f32[1]{0:T(128)S(6)} %copy.10.guide_ref), custom_call_target="tpu_custom_call" | custom-call | tf_op jit(solution)/shard_map/twin_attention/pallas_call | solution.py:287
  41.7 0.6 %copy.9 = bf16[16,1024]{1,0:T(8,128)(2,1)} copy(bf16[16,1024]{1,0:T(8,128)(2,1)S(1)} %twin_attention.1) | data formatting | bytes 65536

commit v10 on v9

--- a/solution.py
+++ b/solution.py
@@ -15,19 +15,6 @@
 MESH = pl.DeviceIdType.MESH
 
 
-def hops(dy, dz):
-    return min(dy, 8 - dy) + min(dz, 8 - dz)
-
-
-AROUND = sorted(
-    ((dy, dz) for dy in range(8) for dz in range(8) if dy or dz), key=lambda d: (-hops(*d), d)
-)
-CLOSE = [d for d in AROUND if hops(*d) <= 5]
-FAR = [d for d in AROUND if hops(*d) > 5]
-FAR_DY = (2, 6, 3, 5, 4)
-FAR_DZ = {dy: [dz for dy2, dz in FAR if dy2 == dy] for dy in FAR_DY}
-
-
 def loop(lo, hi, fn):
     def body(k, carry):
         fn(k)
@@ -44,7 +31,7 @@
     qs_hbm, qc_hbm, k_hbm, v_hbm, pos_hbm, counts_hbm, guide_ref,
     out_ref,
     raw, pos, counts, ones,
-    kv_send, kv_all, q_rot, q_far, q_all, keys_t, o_send, o_recv, l_send, l_recv, merged, paired, scale_here, scale_there,
+    kv_send, kv_all, q_rot, q_y, q_all, keys_t, o_send, o_recv, l_send, l_recv, merged, paired, scale_here, scale_there,
     load_sem, send_sem, recv_sem, kv_sem, qy_sem, qz_sem,
 ):
     cfg = lax.axis_index("cfg")
@@ -85,8 +72,11 @@
 
     barrier = pltpu.get_barrier_semaphore()
 
-    for dy, dz in CLOSE:
-        signal(device(x, (y + dy) % 8, (z + dz) % 8))
+    for k in (4, 3, 5, 2, 6, 1, 7):
+        signal(device(x, (y + k) % 8, tower * 2 + 1 - zl))
+    for k in (4, 3, 5, 2, 6, 1, 7):
+        signal(device(x, (y + k) % 8, z))
+        signal(device(x, y, (z + k) % 8))
     for k in (2, 1, 3):
         signal(device((x + k) % 4, y, z))
     signal({"cfg": 1 - cfg})
@@ -119,7 +109,7 @@
         q_rot[h // 2, 0, h % 2] = rope(0, h).astype(jnp.bfloat16)
         q_rot[h // 2, 1, h % 2] = rope(1, h).astype(jnp.bfloat16)
 
-    pl.semaphore_wait(barrier, len(CLOSE) + 3 + 1)
+    pl.semaphore_wait(barrier, 7 + 7 + 7 + 3 + 1)
 
     own_slot = y * 2 + zl
 
@@ -129,39 +119,33 @@
             device(x, y2, tower * 2 + zl2), 0, kv_sem.at[own_slot],
         )
 
-    def q_for(dy, z2):
-        return q_rot.at[(y + dy) % 8, (z // 6 + z2 // 6) % 2, z2 % 2]
-
-    def place_from(dy):
-        return NEAR.index((8 - dy) % 8)
-
-    def send_q(dy, dz):
-        z2 = (z + dz) % 8
-        block, target = q_all.at[z, place_from(dy)], device(x, (y + dy) % 8, z2)
-        remote(q_for(dy, z2), block, target, 3, qz_sem.at[z])
-
-    def send_far_q(dy, dz):
-        block = q_far.at[FAR.index((dy, dz))]
-        remote(q_for(dy, (z + dz) % 8), block, device(x, (y + dy) % 8, z), 1, qy_sem.at[dy])
-
-    def pass_far_q(dy, dz):
-        block = q_far.at[FAR.index((dy, dz))]
-        target = device(x, y, (z + dz) % 8)
-        remote(block, q_all.at[z, place_from(dy)], target, 3, qz_sem.at[z])
+    def send_q(k):
+        place = NEAR.index((8 - k) % 8)
+        remote(q_rot.at[(y + k) % 8], q_y.at[place], device(x, (y + k) % 8, z), 1, qy_sem.at[place])
 
     def pass_kv(pair):
         for k in (2, 1, 3):
             remote(pair, pair, device((x + k) % 4, y, z), 2, recv_sem.at[2])
 
+    def q_for(z2, places):
+        return q_y.at[places, (z // 6 + z2 // 6) % 2, z2 % 2]
+
+    def pass_q(first, count):
+        places = pl.ds(first, count)
+
+        for k in (4, 3, 5, 2, 6, 1, 7):
+            z2 = (z + k) % 8
+            remote(q_for(z2, places), q_all.at[z, places], device(x, y, z2), 3, qz_sem.at[z])
+
+        local(q_for(z, places), q_all.at[z, places], qz_sem.at[z])
+
+    local(q_rot.at[y], q_y.at[0], qy_sem.at[0])
     for k in (4, 3, 5, 2, 6, 1, 7):
         send_kv((y + k) % 8, zl)
         send_kv((y + k) % 8, 1 - zl)
     send_kv(y, 1 - zl)
-    for dy, dz in FAR:
-        send_far_q(dy, dz)
-    for dy, dz in CLOSE:
-        send_q(dy, dz)
-    local(q_for(0, z), q_all.at[z, 0], qz_sem.at[z])
+    for k in (4, 3, 5, 2, 6, 1, 7):
+        send_q(k)
     local(kv_send.at[own_slot], kv_all.at[x, own_slot], kv_sem.at[own_slot])
 
     def flags(i):
@@ -169,6 +153,7 @@
         ones[i] = jnp.where(row < count, 1.0, 0.0).astype(jnp.bfloat16)
 
     arrived(kv_all.at[x, own_slot], kv_sem.at[own_slot])
+    arrived(q_y.at[0], qy_sem.at[0])
     for place in range(8):
         y2 = (y + NEAR[place]) % 8
         pair = kv_all.at[x, pl.ds(2 * y2, 2)]
@@ -177,10 +162,9 @@
         if place == 0:
             arrived(kv_all.at[x, y * 2 + 1 - zl], kv_sem.at[y * 2 + 1 - zl])
         pass_kv(pair)
-    for dy in FAR_DY:
-        arrived(q_far.at[pl.ds(0, len(FAR_DZ[dy]))], qy_sem.at[dy])
-        for dz in FAR_DZ[dy]:
-            pass_far_q(dy, dz)
+    for place in range(1, 8):
+        arrived(q_y.at[place], qy_sem.at[place])
+    pass_q(0, 8)
     loop(0, 64, flags)
     arrived(kv_all.at[pl.ds(0, 3)], recv_sem.at[2])
 
@@ -272,9 +256,9 @@
         out_ref[:, h * D:(h + 1) * D] = guided.astype(jnp.bfloat16)
 
     sent(kv_send.at[pl.ds(0, 15)], 0)
-    sent(q_far, 1)
+    sent(q_y.at[pl.ds(0, 7)], 1)
     sent(kv_all.at[pl.ds(0, 3)], 2)
-    sent(o_recv.at[pl.ds(0, 63)], 3)
+    sent(q_all.at[pl.ds(0, 7)], 3)
     sent(o_recv.at[pl.ds(0, 63)], 4)
     sent(l_recv.at[pl.ds(0, 63)], 5)
     sent(paired, 6)
@@ -297,7 +281,7 @@
             pltpu.VMEM((HEADS, 2, TOK, D), bf16),
             pltpu.VMEM((4, HEADS, 2, TOK, D), bf16),
             pltpu.VMEM((8, 2, 2, TOK, D), bf16),
-            pltpu.VMEM((len(FAR), TOK, D), bf16),
+            pltpu.VMEM((8, 2, 2, TOK, D), bf16),
             pltpu.VMEM((8, 8, TOK, D), bf16),
             pltpu.VMEM((D, 64 * TOK), bf16),
             pltpu.VMEM((8, 8, TOK, D), bf16),

time: 42.5 us -> 41.8 us (0.984)
  Pallas kernels: 41.1 us -> 40.4 us
    pallas_call x1, Pallas kernels: 41.1 us -> 40.4 us  [per_device(): pl.pallas_call(kernel, out_shape=pltpu.VMEM((TOK, HEADS * D // 2), bf16),...]
where the time goes in v10:
time: 41.8 us; the launch traced here: 41.7 us
  Pallas kernels  40.4 us (97%)
  between operations  0.66 us (2%)
  local copies, waits for them, and re-layouts  0.62 us (1%)
    pallas_call x1, Pallas kernels, per_device(): pl.pallas_call(kernel, out_shape=pltpu.VMEM((TOK, HEADS * D // 2), bf16),...  40.4 us

profile of v10, /device:TPU:1, one launch (start us, length us, event | category | flops | bytes accessed | tf_op | source)
XLA Modules:
  0.0 41.7 jit_solution(4952811879656926766)
XLA Ops:
  0.7 40.4 %twin_attention.1 = bf16[16,1024]{1,0:T(8,128)(2,1)S(1)} custom-call(bf16[16,2048]{1,0:T(8,128)(2,1)} %bitcast.4, bf16[16,2048]{1,0:T(8,128)(2,1)} %bitcast.5, bf16[16,2048]{1,0:T(8,128)(2,1)} %bitcast.6, bf16[16,2048]{1,0:T(8,128)(2,1)} %bitcast.7, s32[16]{0:T(128)} %pos_hbm.1, s32[256]{0:T(256)} %counts_hbm.1, f32[1]{0:T(128)S(6)} %copy.10.guide_ref), custom_call_target="tpu_custom_call" | custom-call | tf_op jit(solution)/shard_map/twin_attention/pallas_call | solution.py:271
  41.0 0.6 %copy.9 = bf16[16,1024]{1,0:T(8,128)(2,1)} copy(bf16[16,1024]{1,0:T(8,128)(2,1)S(1)} %twin_attention.1) | data formatting | bytes 65536

commit v11 on v10

--- a/solution.py
+++ b/solution.py
@@ -32,7 +32,7 @@
     out_ref,
     raw, pos, counts, ones,
     kv_send, kv_all, q_rot, q_y, q_all, keys_t, o_send, o_recv, l_send, l_recv, merged, paired, scale_here, scale_there,
-    load_sem, send_sem, recv_sem, kv_sem, qy_sem, qz_sem,
+    load_sem, send_sem, recv_sem, kv_sem, qy_sem, qz_sem, x_sem,
 ):
     cfg = lax.axis_index("cfg")
     tower = lax.axis_index("tower")
@@ -125,7 +125,7 @@
 
     def pass_kv(pair):
         for k in (2, 1, 3):
-            remote(pair, pair, device((x + k) % 4, y, z), 2, recv_sem.at[2])
+            remote(pair, pair, device((x + k) % 4, y, z), 2, x_sem.at[x])
 
     def q_for(z2, places):
         return q_y.at[places, (z // 6 + z2 // 6) % 2, z2 % 2]
@@ -166,17 +166,25 @@
         arrived(q_y.at[place], qy_sem.at[place])
     pass_q(0, 8)
     loop(0, 64, flags)
-    arrived(kv_all.at[pl.ds(0, 3)], recv_sem.at[2])
+
+    def turn(x2):
+        keys_t[x2] = jnp.transpose(kv_all[x2, :, 0].reshape(16 * TOK, D))
+
+    turn(x)
+    for k in (1, 3, 2):
+        x2 = (x + k) % 4
+        arrived(kv_all.at[x2], x_sem.at[x2])
+        turn(x2)
 
     slot = tower * HEADS + own_slot
-    keys_t[...] = jnp.transpose(kv_all[:, :, 0].reshape(64 * TOK, D))
 
     def attend(z2):
         queries = q_all[z2].reshape(8 * TOK, D)
+        keys = jnp.concatenate([keys_t[i] for i in range(4)], axis=1)
         values = jnp.concatenate(
             [kv_all[:, :, 1].reshape(64 * TOK, D), ones[...].reshape(64 * TOK, D)], axis=1
         )
-        scores = jnp.dot(queries, keys_t[...], preferred_element_type=jnp.float32)
+        scores = jnp.dot(queries, keys, preferred_element_type=jnp.float32)
         highest = jnp.max(scores, axis=1, keepdims=True)
         weights = jnp.exp2((scores - highest) * (SCALE / math.log(2.0))).astype(jnp.bfloat16)
         total = jnp.dot(weights, values, preferred_element_type=jnp.float32)
@@ -283,7 +291,7 @@
             pltpu.VMEM((8, 2, 2, TOK, D), bf16),
             pltpu.VMEM((8, 2, 2, TOK, D), bf16),
             pltpu.VMEM((8, 8, TOK, D), bf16),
-            pltpu.VMEM((D, 64 * TOK), bf16),
+            pltpu.VMEM((4, D, 16 * TOK), bf16),
             pltpu.VMEM((8, 8, TOK, D), bf16),
             pltpu.VMEM((64, TOK, D), bf16),
             pltpu.VMEM((8, 1, D), jnp.float32),
@@ -298,6 +306,7 @@
             pltpu.SemaphoreType.DMA((16,)),
             pltpu.SemaphoreType.DMA((8,)),
             pltpu.SemaphoreType.DMA((8,)),
+            pltpu.SemaphoreType.DMA((4,)),
         ],
         compiler_params=pltpu.CompilerParams(
             collective_id=0, has_side_effects=True, vmem_limit_bytes=56 * 1024 * 1024

time: 41.8 us -> 41.9 us (level)
  no operation moved by 1% of the time
where the time goes in v11:
time: 41.9 us; the launch traced here: 41.7 us
  Pallas kernels  40.4 us (96%)
  between operations  0.66 us (2%)
  local copies, waits for them, and re-layouts  0.62 us (1%)
    pallas_call x1, Pallas kernels, per_device(): pl.pallas_call(kernel, out_shape=pltpu.VMEM((TOK, HEADS * D // 2), bf16),...  40.4 us

profile of v11, /device:TPU:1, one launch (start us, length us, event | category | flops | bytes accessed | tf_op | source)
XLA Modules:
  0.0 41.7 jit_solution(2176877096342492275)
XLA Ops:
  0.7 40.4 %twin_attention.1 = bf16[16,1024]{1,0:T(8,128)(2,1)S(1)} custom-call(bf16[16,2048]{1,0:T(8,128)(2,1)} %bitcast.4, bf16[16,2048]{1,0:T(8,128)(2,1)} %bitcast.5, bf16[16,2048]{1,0:T(8,128)(2,1)} %bitcast.6, bf16[16,2048]{1,0:T(8,128)(2,1)} %bitcast.7, s32[16]{0:T(128)} %pos_hbm.1, s32[256]{0:T(256)} %counts_hbm.1, f32[1]{0:T(128)S(6)} %copy.10.guide_ref), custom_call_target="tpu_custom_call" | custom-call | tf_op jit(solution)/shard_map/twin_attention/pallas_call | solution.py:279
  41.1 0.6 %copy.9 = bf16[16,1024]{1,0:T(8,128)(2,1)} copy(bf16[16,1024]{1,0:T(8,128)(2,1)S(1)} %twin_attention.1) | data formatting | bytes 65536
